TPU v7x, 256 devices: a whole 4x4x8 slice. The times are simulated.
256 devices in a mesh: seq: 32 (over x, y, core), ch: 8 (over z).
Axes of the slice: x: 4, y: 4, z: 8, core: 2. Of those that a mesh axis runs over, the one named last changes fastest.
Arguments:
- query_in: bfloat16 [16384, 8192], P('seq', 'ch'), may hold values from -6 to 6
- key_in: bfloat16 [16384, 8192], P('seq', 'ch'), may hold values from -6 to 6
- value_in: bfloat16 [16384, 8192], P('seq', 'ch'), may hold values from -6 to 6
- short_weight: float32 [3, 3, 8192], P(None, None, 'ch'), may hold values from -3 to 3
- skip_bias: float32 [8192], P('ch'), may hold values from -4 to 4
- filter_taps: float32 [512, 16384], P('ch', 'seq'), may hold values from -0.046875 to 0.046875
Outputs:
- hyena_out: bfloat16 [16384, 8192], P('seq', 'ch')
All inputs are finite; a program needn't handle non-finite values.
Results may differ from a plain program's by a relative error of at most 0.001.
Values may be sent and summed in bfloat16 or wider, within the bound.
No kernel may reach another device: no remote copies, remote signals or barrier semaphores. Data moves between devices by JAX's collectives and lax.ppermute only.
A program may use at most 192 MiB of HBM per device.

v0:
```python
import math

import jax
import jax.numpy as jnp
import numpy as np
from jax import lax
from jax.experimental import pallas as pl
from jax.experimental.pallas import tpu as pltpu
from jax.sharding import PartitionSpec as P

GROUP_SIZE = 16
SIDE = 128
LANES = 128
WIDE = 4
CODE_SPAN = 240.0
CODE_TOP = 4096.0
CODE_GAIN = CODE_SPAN / math.log2(1.0 + CODE_TOP)
INV_LN2 = 1.0 / math.log(2.0)
RESIDENT_LIMIT = 12 * 1024 * 1024
STREAMING_LIMIT = 60 * 1024 * 1024

f32, bf16 = jnp.float32, jnp.bfloat16


def encode(value, to_units):
    level = jnp.log(1.0 + jnp.abs(value) * to_units) * (CODE_GAIN * INV_LN2)
    code = jnp.exp2(level - CODE_SPAN / 2)
    return jnp.where(value < 0, -code, code)


def decode(code, from_units):
    level = jnp.log(jnp.abs(code)) * (INV_LN2 / CODE_GAIN)
    size = (jnp.exp2(level + CODE_SPAN / 2 / CODE_GAIN) - 1.0) * from_units
    return jnp.where(code < 0, -size, size)


def code_scale(largest):
    return (jnp.maximum(largest, 1e-30) * 1.01).astype(bf16).astype(f32)


def tables():
    side = np.arange(SIDE)
    inner = 2 * np.pi / SIDE * (side[:, None] * side[None, :] % SIDE)
    outer = 2 * np.pi / (4 * SIDE) * (side[None, :] * (4 * side[:, None] + 1) % (4 * SIDE))
    twist = 2 * np.pi / (4 * SIDE * SIDE) * (side[None, :] * (4 * side[:, None] + 1))
    first = np.concatenate([np.cos(outer), -np.sin(outer)], axis=0)
    second = np.block([[np.cos(inner), -np.sin(inner)], [np.sin(inner), np.cos(inner)]])
    third = np.block([[np.cos(inner), np.sin(inner)], [-np.sin(inner), np.cos(inner)]])
    fourth = np.concatenate([np.cos(outer).T, -np.sin(outer).T], axis=1)

    def parts(table):
        high = table.astype(jnp.bfloat16)
        return high, (table - high.astype(np.float64)).astype(jnp.bfloat16)

    def beside(table):
        high, low = parts(table)
        return np.concatenate([high, high, low], axis=0)

    return (
        np.concatenate([np.concatenate([part, part], axis=1) for part in parts(first)], axis=0),
        beside(second),
        beside(third),
        np.concatenate(parts(fourth), axis=0),
        np.stack([np.cos(twist), np.sin(twist)]).astype(np.float32),
    )


def dot(left, right):
    return jnp.dot(left, right, preferred_element_type=f32)


def halves(value):
    high = value.astype(bf16)
    return high, (value - high.astype(f32)).astype(bf16)


def short_conv(stream, at, lanes, before, weights, padded):
    now = stream[pl.ds(at, SIDE), lanes].astype(f32)
    padded[8:16, :] = before
    padded[16:, :] = now
    return (
        weights[0:1] * now
        + weights[1:2] * padded[15 : 15 + SIDE, :]
        + weights[2:3] * padded[14 : 14 + SIDE, :]
    )


def gate_kernel(
    q_hbm,
    k_hbm,
    v_hbm,
    w_hbm,
    taps_hbm,
    out_hbm,
    k_buf,
    v_buf,
    q_buf,
    w_buf,
    taps_buf,
    out_ref,
    pads,
    scales,
    ends,
    q_ends,
    taps_in,
    sems,
):
    rows, channels = k_buf.shape
    steps = rows // SIDE
    blocks = channels // LANES
    dests = out_ref.shape[0] // blocks
    per = LANES // dests
    base = steps * per
    held = taps_buf.shape[0] // blocks
    groups = held // dests

    def stream_copy(at, step):
        source, target = ((k_hbm, k_buf), (v_hbm, v_buf))[at]
        span = pl.ds(step * SIDE, SIDE)
        return pltpu.make_async_copy(source.at[span], target.at[span], sems.at[at, step])

    def out_copy(step):
        end = base + 16 if step == steps - 1 else (step + 1) * per
        span = pl.ds(step * per, end - step * per)
        return pltpu.make_async_copy(out_ref.at[:, span], out_hbm.at[:, span], sems.at[3, step])

    w_copy = pltpu.make_async_copy(w_hbm, w_buf, sems.at[2, 0])
    taps_copy = pltpu.make_async_copy(taps_hbm, taps_buf, sems.at[2, 1])
    q_copy = pltpu.make_async_copy(q_hbm.at[pl.ds(rows - 16, 16)], q_buf, sems.at[2, 2])
    for step in range(steps):
        for at in range(2):
            stream_copy(at, step).start()
        if step == 0:
            w_copy.start()
    taps_copy.start()
    q_copy.start()
    w_copy.wait()

    for step in range(steps):
        for at in range(2):
            stream_copy(at, step).wait()

        def tile(block, slot, step=step):
            lanes = pl.ds(pl.multiple_of(block * LANES, LANES), LANES)
            shorts = []
            for at, buf in enumerate((k_buf, v_buf)):
                if step == 0:
                    before = jnp.zeros((8, LANES), f32)
                else:
                    before = buf[step * SIDE - 16 : step * SIDE, lanes].astype(f32)[8:]
                shorts.append(
                    short_conv(
                        buf, step * SIDE, lanes, before, w_buf[1 + at, :, lanes], pads.at[slot, at]
                    )
                )
            gated = shorts[0] * shorts[1]
            scale = code_scale(jnp.max(jnp.abs(gated), axis=0, keepdims=True))
            scales[step : step + 1, lanes] = scale
            code = encode(gated, CODE_TOP / scale).T.astype(bf16)
            first = pl.multiple_of(block * dests, dests)
            out_ref[pl.ds(first, dests), step * per : (step + 1) * per, :] = code.reshape(
                dests, per, LANES
            )

        def tiles(n, carry):
            tile(2 * n, 0)
            tile(2 * n + 1, 1)
            return carry

        lax.fori_loop(0, blocks // 2, tiles, 0)
        if step < steps - 1:
            out_copy(step).start()

    taps_copy.wait()
    q_copy.wait()

    def tail(block, slot):
        lanes = pl.ds(pl.multiple_of(block * LANES, LANES), LANES)
        for a in range(steps):
            taps_in[slot, a * held : (a + 1) * held, :] = taps_buf[
                pl.ds(pl.multiple_of(block * held, held), held), a * LANES : (a + 1) * LANES
            ]
        taps_at = steps * held
        for a in range(steps):
            for g in range(groups):
                piece = taps_in[slot, pl.ds(a * held + g, dests, stride=groups), :]
                taps_in[slot, pl.ds(taps_at + a * groups + g, dests, stride=8), :] = piece
        own_taps = taps_in[slot, taps_at:, :]
        taps_scale = code_scale(jnp.max(jnp.abs(own_taps), axis=1, keepdims=True))
        taps_code = encode(own_taps, CODE_TOP / taps_scale)
        taps_scale = jnp.broadcast_to(taps_scale, own_taps.shape)
        for at, buf in enumerate((k_buf, v_buf)):
            ends[slot, 4 * at : 4 * at + 2, :] = buf[rows - 16 :, lanes].astype(f32)[14:16]
            ends[slot, 4 * at + 2 : 4 * at + 4, :] = buf[0:16, lanes].astype(f32)[0:2]
        q_ends[slot, 0:2, :] = q_buf[:, lanes].astype(f32)[14:16]
        lane = lax.broadcasted_iota(jnp.int32, (8, LANES), 1)
        for d in range(dests):
            asked = pltpu.roll(q_ends[slot], (LANES + 3 * per - d * per) % LANES, 1)
            kept = pltpu.roll(ends[slot], (LANES - d * per) % LANES, 1)
            scaled = pltpu.roll(scales[:, lanes], (LANES + per - d * per) % LANES, 1)
            of_taps = taps_scale[8 * d : 8 * d + 8]
            last = jnp.where(lane < per, kept, jnp.where(lane < 2 * per, scaled, of_taps))
            last = jnp.where(lane < 3 * per, last, asked)
            both = jnp.concatenate([taps_code[8 * d : 8 * d + 8], last], axis=0).astype(bf16)
            out_ref[block * dests + d, base : base + 16, :] = both

    def tails(n, carry):
        tail(2 * n, 0)
        tail(2 * n + 1, 1)
        return carry

    scales[steps:, :] = jnp.zeros((8 - steps, channels), f32)
    q_ends[...] = jnp.zeros_like(q_ends)
    lax.fori_loop(0, blocks // 2, tails, 0)
    out_copy(steps - 1).start()
    for step in range(steps):
        out_copy(step).wait()


def mix_kernel(
    in_hbm,
    w_hbm,
    first_hbm,
    second_hbm,
    third_hbm,
    fourth_hbm,
    twist_hbm,
    out_hbm,
    in_ref,
    w_ref,
    first,
    second,
    third,
    fourth,
    twist,
    out_ref,
    signal_0,
    signal_1,
    result_0,
    result_1,
    taps,
    spectra,
    largest,
    units,
    tails,
    back_tails,
    levels,
    starts,
    turned,
    filtered,
    unturned,
    in_sems,
    table_sems,
    out_sems,
):
    signals, results = (signal_0, signal_1), (result_0, result_1)
    groups = len(signals)
    blocks = in_ref.shape[0]
    per_block = SIDE // blocks
    channels = groups * GROUP_SIZE
    data = per_block * channels
    count = channels // WIDE
    slots = count // groups
    slot_blocks = blocks // slots

    def in_copy(slot):
        span = pl.ds(slot * slot_blocks, slot_blocks)
        return pltpu.make_async_copy(in_hbm.at[span], in_ref.at[span], in_sems.at[slot])

    def out_copy(slot):
        span = pl.ds(slot * slot_blocks, slot_blocks)
        return pltpu.make_async_copy(out_ref.at[span], out_hbm.at[span], out_sems.at[slot])

    table_copies = [
        pltpu.make_async_copy(source, target, table_sems.at[at])
        for at, (source, target) in enumerate(
            (
                (w_hbm, w_ref),
                (twist_hbm, twist),
                (first_hbm, first),
                (second_hbm, second),
                (third_hbm, third),
                (fourth_hbm, fourth),
            )
        )
    ]
    for slot in range(slots):
        in_copy(slot).start()
    for copy in table_copies:
        copy.start()

    lane = lax.broadcasted_iota(jnp.int32, (GROUP_SIZE, LANES), 1)

    def start_of(j, group):
        return starts[j * channels + group * GROUP_SIZE : j * channels + (group + 1) * GROUP_SIZE, :]

    def unpack(slot, group, with_starts):
        for i in range(slot_blocks):
            j = slot * slot_blocks + i
            for a in range(per_block):
                at = a * channels + group * GROUP_SIZE
                value = decode(in_ref[j, at : at + GROUP_SIZE, :].astype(f32), 1.0)
                if a == 0 and with_starts:
                    value = jnp.where(lane < 2, start_of(j, group), value)
                place = (j * per_block + a) * GROUP_SIZE
                signals[group][place : place + GROUP_SIZE, :] = value

    for slot in range(slots):
        in_copy(slot).wait()
        unpack(slot, 0, False)
    table_copies[0].wait()

    of_message = in_ref[:, data : data + 16, :].astype(f32)
    tails[...] = of_message[:, 8:].reshape(blocks * 8, LANES)
    taps_code = of_message[:, :8].reshape(blocks * 8, LANES)
    taps[...] = decode(taps_code, 1.0 / CODE_TOP) * tails[:, 2 * channels : 2 * channels + 1]
    for a in range(per_block):
        levels[pl.ds(a, blocks, stride=per_block), :] = tails[pl.ds(a, blocks, stride=8), :]

    def gated_starts():
        block = lax.broadcasted_iota(jnp.int32, (blocks, LANES), 0)
        lanes = lax.broadcasted_iota(jnp.int32, (blocks, LANES), 1)
        shorts = []
        for at in range(2):
            ago_2, ago_1, now, later = [
                tails[pl.ds(4 * at + i, blocks, stride=8), :] for i in range(4)
            ]
            ago_2 = jnp.where(block == 0, 0.0, pltpu.roll(ago_2, 1, 0))
            ago_1 = jnp.where(block == 0, 0.0, pltpu.roll(ago_1, 1, 0))
            back_tails[pl.ds(3 + 2 * at, blocks, stride=8), :] = ago_2
            back_tails[pl.ds(4 + 2 * at, blocks, stride=8), :] = ago_1
            taps_0, taps_1, taps_2 = [w_ref[1 + at, i : i + 1, :] for i in range(3)]
            shorts.append(
                (
                    taps_0 * now + taps_1 * ago_1 + taps_2 * ago_2,
                    taps_0 * later + taps_1 * now + taps_2 * ago_1,
                )
            )
        for at in range(2):
            asked = pltpu.roll(tails[pl.ds(at, blocks, stride=8), :], LANES - 3 * channels, 1)
            asked = jnp.where(block == 0, 0.0, pltpu.roll(asked, 1, 0))
            back_tails[pl.ds(1 + at, blocks, stride=8), :] = asked
        level = pltpu.roll(tails[pl.ds(0, blocks, stride=8), :], LANES - channels, 1)
        to_level = CODE_TOP / jnp.where(lanes < channels, level, 1.0)
        packed = jnp.zeros((blocks, LANES), f32)
        for token in range(2):
            parts = halves(shorts[0][token] * shorts[1][token] * to_level)
            for at, part in enumerate(parts):
                place = 2 * token + at
                moved = pltpu.roll(part.astype(f32), place * channels, 1)
                packed = jnp.where(lanes // channels == place, moved, packed)
        lane = lax.broadcasted_iota(jnp.int32, (blocks, channels, LANES), 2)
        row = lax.broadcasted_iota(jnp.int32, (blocks, channels, LANES), 1)
        picked = jnp.where(lane % channels == row, packed[:, None, :], 0.0).astype(bf16)
        from_lane = lax.broadcasted_iota(jnp.int32, (LANES, LANES), 0)
        to_lane = lax.broadcasted_iota(jnp.int32, (LANES, LANES), 1)
        place = jnp.where(from_lane // (2 * channels) == to_lane, 1.0, 0.0).astype(bf16)
        starts[...] = dot(picked.reshape(blocks * channels, LANES), place)

    gated_starts()
    for j in range(blocks):
        place = j * per_block * GROUP_SIZE
        span = slice(place, place + GROUP_SIZE)
        signal_0[span, :] = jnp.where(lane < 2, start_of(j, 0), signal_0[span, :])
    for copy in table_copies[1:]:
        copy.wait()

    cos, sin = twist[0], twist[1]

    def store_halves(ref, at, value):
        high, low = halves(value)
        ref[at * SIDE : (at + 1) * SIDE, : 2 * SIDE] = high
        ref[at * SIDE : (at + 1) * SIDE, 2 * SIDE :] = low

    def table_right(ref, table, used=WIDE):
        rows = used * SIDE
        return dot(ref[:rows], table[: 4 * SIDE]) + dot(ref[:rows, : 2 * SIDE], table[4 * SIDE :])

    def first_side(values):
        for pair in range(len(values) // 2):
            high, low = halves(jnp.concatenate(values[2 * pair : 2 * pair + 2], axis=1))
            wide = dot(first[...], jnp.concatenate([high, low], axis=0))
            wide = wide[: 2 * SIDE] + wide[2 * SIDE :]
            for at in range(2):
                re = wide[:SIDE, at * SIDE : (at + 1) * SIDE]
                im = wide[SIDE:, at * SIDE : (at + 1) * SIDE]
                store_halves(
                    turned,
                    2 * pair + at,
                    jnp.concatenate([re * cos + im * sin, im * cos - re * sin], axis=1),
                )

    def load(n, group):
        level = pltpu.roll(levels[...], LANES - channels - WIDE * n, 1) * (1.0 / CODE_TOP)
        at = WIDE * (n - group * slots)
        return [
            signals[group][pl.ds(at + i, SIDE, stride=GROUP_SIZE), :] * level[:, i : i + 1]
            for i in range(WIDE)
        ]

    def second_side(n):
        spectrum = table_right(turned, second)
        of_taps = spectra[WIDE * n // GROUP_SIZE]
        f_re, f_im = of_taps[:, :SIDE], of_taps[:, SIDE:]
        for at in range(WIDE):
            s_re = spectrum[at * SIDE : (at + 1) * SIDE, :SIDE]
            s_im = spectrum[at * SIDE : (at + 1) * SIDE, SIDE:]
            store_halves(
                filtered,
                at,
                jnp.concatenate([s_re * f_re - s_im * f_im, s_re * f_im + s_im * f_re], axis=1),
            )

    def second_side_back():
        back = table_right(filtered, third)
        for at in range(WIDE):
            re = back[at * SIDE : (at + 1) * SIDE, :SIDE]
            im = back[at * SIDE : (at + 1) * SIDE, SIDE:]
            high, low = halves(jnp.concatenate([re * cos - im * sin, im * cos + re * sin], axis=0))
            unturned[: 2 * SIDE, at * SIDE : (at + 1) * SIDE] = high
            unturned[2 * SIDE :, at * SIDE : (at + 1) * SIDE] = low

    def first_side_back(n, group):
        for pair in range(WIDE // 2):
            span = slice(2 * pair * SIDE, (2 * pair + 2) * SIDE)
            done = dot(fourth[...], unturned[: 2 * SIDE, span])
            done = done[:SIDE] + done[SIDE:] + dot(fourth[:SIDE], unturned[2 * SIDE :, span])
            top = jnp.max(jnp.abs(done), axis=0, keepdims=True)
            for i in range(2):
                span = slice(i * SIDE, (i + 1) * SIDE)
                at = WIDE * n + 2 * pair + i
                place = pl.ds(at - group * GROUP_SIZE, SIDE, stride=GROUP_SIZE)
                results[group][place, :] = done[:, span]
                largest[pl.ds(at, 1), :] = top[:, span]

    def scale_group(group):
        span = slice(group * GROUP_SIZE, (group + 1) * GROUP_SIZE)
        scale = code_scale(jnp.max(largest[span, :], axis=1, keepdims=True))
        units[span, :] = jnp.broadcast_to(scale, (GROUP_SIZE, LANES))

    def pack(slot, group):
        to_units = CODE_TOP / units[group * GROUP_SIZE : (group + 1) * GROUP_SIZE, :]
        for i in range(slot_blocks):
            j = slot * slot_blocks + i
            for a in range(per_block):
                at = a * channels + group * GROUP_SIZE
                place = (j * per_block + a) * GROUP_SIZE
                value = results[group][place : place + GROUP_SIZE, :]
                out_ref[j, at : at + GROUP_SIZE, :] = encode(value, to_units).astype(bf16)

    def step(n, carry):
        first_side_back(n - 3, 0)
        second_side_back()
        second_side(n - 1)
        first_side(load(n, 1))
        return carry

    first_side([taps[pl.ds(g, SIDE, stride=groups), :] for g in range(groups)])
    spectra[...] = table_right(turned, second, groups).reshape(groups, SIDE, 2 * SIDE) * (
        1.0 / (SIDE * SIDE)
    )
    first_side(load(0, 0))
    unpack(0, 1, True)
    second_side(0)
    first_side(load(1, 0))
    unpack(1, 1, True)
    second_side_back()
    second_side(1)
    first_side(load(2, 0))
    unpack(2, 1, True)
    first_side_back(0, 0)
    second_side_back()
    second_side(2)
    first_side(load(3, 0))
    unpack(3, 1, True)
    lax.fori_loop(4, 7, step, 0)
    scale_group(0)
    pack(0, 0)
    first_side_back(4, 1)
    second_side_back()
    second_side(6)
    first_side(load(7, 1))
    pack(1, 0)
    first_side_back(5, 1)
    second_side_back()
    second_side(7)
    pack(2, 0)
    first_side_back(6, 1)
    second_side_back()
    pack(3, 0)
    first_side_back(7, 1)
    scale_group(1)

    diagonal = lax.broadcasted_iota(jnp.int32, (channels, LANES), 1) == lax.broadcasted_iota(
        jnp.int32, (channels, LANES), 0
    )
    scale_row = jnp.sum(jnp.where(diagonal, units[...], 0.0), axis=0, keepdims=True)
    back_tails[pl.ds(0, blocks, stride=8), :] = jnp.broadcast_to(scale_row, (blocks, LANES))
    back_tails[pl.ds(7, blocks, stride=8), :] = jnp.zeros((blocks, LANES), f32)
    out_ref[:, data : data + 8, :] = back_tails[...].reshape(blocks, 8, LANES).astype(bf16)
    for slot in range(slots):
        pack(slot, 1)
        out_copy(slot).start()
    for slot in range(slots):
        out_copy(slot).wait()


def local_kernel(q_ref, k_ref, v_ref, w_ref, skip_ref, q_out, s_out, ends_out, pads):
    rows, channels = q_ref.shape

    def column(block, carry):
        lanes = pl.ds(pl.multiple_of(block * LANES, LANES), LANES)
        for step in range(rows // SIDE):
            shorts = []
            for at, ref in enumerate((q_ref, k_ref, v_ref)):
                if step == 0:
                    before = jnp.zeros((8, LANES), f32)
                else:
                    before = ref[step * SIDE - 16 : step * SIDE, lanes].astype(f32)[8:]
                shorts.append(
                    short_conv(ref, step * SIDE, lanes, before, w_ref[at, :, lanes], pads.at[at])
                )
            if step == 0:
                ends_out[0:2, lanes] = shorts[1][0:2]
                ends_out[2:4, lanes] = shorts[2][0:2]
            span = slice(step * SIDE, (step + 1) * SIDE)
            q_out[span, lanes] = shorts[0]
            s_out[span, lanes] = skip_ref[:, lanes] * (shorts[1] * shorts[2])
        return carry

    ends_out[...] = jnp.zeros_like(ends_out)
    lax.fori_loop(0, channels // LANES, column, 0)


def join_kernel(
    in_ref, q_ref, s_ref, ends_ref, w_ref, skip_ref, out_hbm, out_buf, units, fixes, sems
):
    rows, channels = q_ref.shape
    blocks = channels // LANES
    sources = in_ref.shape[0] // blocks
    per = LANES // sources
    steps = rows // SIDE
    base = steps * per
    lane = lax.broadcasted_iota(jnp.int32, (8, LANES), 1)
    for block in range(blocks):
        lanes = slice(block * LANES, (block + 1) * LANES)
        tail = jnp.zeros((8, LANES), f32)
        for i in range(sources):
            part = in_ref[block * sources + i, base : base + 8, :].astype(f32)
            tail = jnp.where(lane // per == i, pltpu.roll(part, i * per, 1), tail)
        units[:, lanes] = tail[0:1] * (1.0 / CODE_TOP)
        adds = []
        for at in range(3):
            ago_2, ago_1 = tail[1 + 2 * at : 2 + 2 * at], tail[2 + 2 * at : 3 + 2 * at]
            weight_1, weight_2 = w_ref[at, 1:2, lanes], w_ref[at, 2:3, lanes]
            adds.append((weight_1 * ago_1 + weight_2 * ago_2, weight_2 * ago_1))
        for token in range(2):
            k_short = ends_ref[token : token + 1, lanes] + adds[1][token]
            v_short = ends_ref[2 + token : 3 + token, lanes] + adds[2][token]
            fixes[token : token + 1, lanes] = q_ref[token : token + 1, lanes] + adds[0][token]
            fixes[2 + token : 3 + token, lanes] = skip_ref[:, lanes] * (k_short * v_short)

    first_rows = lax.broadcasted_iota(jnp.int32, (8, LANES), 0) < 2
    copies = []
    for step in range(steps):
        span = slice(step * SIDE, (step + 1) * SIDE)

        def column(block, carry, step=step, span=span):
            lanes = pl.ds(pl.multiple_of(block * LANES, LANES), LANES)
            first = pl.multiple_of(block * sources, sources)
            code = in_ref[pl.ds(first, sources), step * per : (step + 1) * per, :]
            tile = code.astype(f32).reshape(LANES, SIDE).T
            long_conv = decode(tile, units[:, lanes])
            q_short, skipped = q_ref[span, lanes], s_ref[span, lanes]
            if step == 0:
                fix = fixes[:, lanes]
                q_start = jnp.where(first_rows, fix, q_short[:8])
                s_start = jnp.where(first_rows, pltpu.roll(fix, 6, 0), skipped[:8])
                q_short = jnp.concatenate([q_start, q_short[8:]], axis=0)
                skipped = jnp.concatenate([s_start, skipped[8:]], axis=0)
            out_buf[span, lanes] = (q_short * (long_conv + skipped)).astype(bf16)
            return carry

        lax.fori_loop(0, blocks, column, 0, unroll=2)
        rows_at = pl.ds(step * SIDE, SIDE)
        copies.append(
            pltpu.make_async_copy(out_buf.at[rows_at], out_hbm.at[rows_at], sems.at[step])
        )
        copies[-1].start()
    for copy in copies:
        copy.wait()


def shards(query_in, key_in, value_in, short_weight, skip_bias, filter_taps):
    rows, channels = query_in.shape
    seq = lax.axis_size("seq")
    own = channels // seq
    blocks = channels // LANES
    groups = own // GROUP_SIZE
    sent = rows * own // LANES
    steps = rows // SIDE
    whole = pl.BlockSpec(memory_space=pltpu.VMEM)
    hbm = pl.BlockSpec(memory_space=pltpu.HBM)
    resident = pltpu.CompilerParams(vmem_limit_bytes=RESIDENT_LIMIT)
    streaming = pltpu.CompilerParams(vmem_limit_bytes=STREAMING_LIMIT)

    message = pl.pallas_call(
        gate_kernel,
        in_specs=[hbm] * 5,
        out_specs=hbm,
        out_shape=jax.ShapeDtypeStruct((seq, sent + 16, LANES), bf16),
        scratch_shapes=[
            pltpu.VMEM((rows, channels), bf16),
            pltpu.VMEM((rows, channels), bf16),
            pltpu.VMEM((16, channels), bf16),
            pltpu.VMEM(short_weight.shape, f32),
            pltpu.VMEM(filter_taps.shape, f32),
            pltpu.VMEM((seq, sent + 16, LANES), bf16),
            pltpu.VMEM((2, 2, 16 + SIDE, LANES), f32),
            pltpu.VMEM((8, channels), f32),
            pltpu.VMEM((2, 8, LANES), f32),
            pltpu.VMEM((2, 8, LANES), f32),
            pltpu.VMEM((2, 2 * steps * filter_taps.shape[0] // blocks, LANES), f32),
            pltpu.SemaphoreType.DMA((4, steps)),
        ],
        compiler_params=streaming,
        name="gate",
    )(query_in, key_in, value_in, short_weight, filter_taps)
    message, query_in, key_in, value_in, short_weight, skip_bias, *known = lax.optimization_barrier(
        (message, query_in, key_in, value_in, short_weight, skip_bias, *tables())
    )
    message = lax.all_to_all(message, "seq", 0, 0)

    q_short, skipped, ends = pl.pallas_call(
        local_kernel,
        in_specs=[whole] * 5,
        out_specs=[whole] * 3,
        out_shape=[
            jax.ShapeDtypeStruct((rows, channels), f32),
            jax.ShapeDtypeStruct((rows, channels), f32),
            jax.ShapeDtypeStruct((8, channels), f32),
        ],
        scratch_shapes=[pltpu.VMEM((3, 16 + SIDE, LANES), f32)],
        compiler_params=resident,
        cost_estimate=pl.CostEstimate(
            flops=20 * rows * channels, bytes_accessed=14 * rows * channels, transcendentals=0
        ),
        name="local",
    )(query_in, key_in, value_in, short_weight, skip_bias[None])
    weights = lax.dynamic_slice_in_dim(short_weight, lax.axis_index("seq") * own, own, axis=2)
    weights = jnp.pad(weights, ((0, 0), (0, 0), (0, LANES - own)))
    message, q_short, skipped, ends, weights = lax.optimization_barrier(
        (message, q_short, skipped, ends, weights)
    )

    table_shapes = [pltpu.VMEM(table.shape, table.dtype) for table in known]
    message = pl.pallas_call(
        mix_kernel,
        in_specs=[hbm] * 7,
        out_specs=hbm,
        out_shape=jax.ShapeDtypeStruct((seq, sent + 8, LANES), bf16),
        scratch_shapes=[
            pltpu.VMEM((seq, sent + 16, LANES), bf16),
            pltpu.VMEM(weights.shape, f32),
            *table_shapes,
            pltpu.VMEM((seq, sent + 8, LANES), bf16),
            *[pltpu.VMEM((seq * sent // groups, LANES), f32)] * (2 * groups),
            pltpu.VMEM((seq * 8, LANES), f32),
            pltpu.VMEM((groups, SIDE, 2 * SIDE), f32),
            pltpu.VMEM((own, LANES), f32),
            pltpu.VMEM((own, LANES), f32),
            pltpu.VMEM((seq * 8, LANES), f32),
            pltpu.VMEM((seq * 8, LANES), f32),
            pltpu.VMEM((SIDE, LANES), f32),
            pltpu.VMEM((seq * own, LANES), f32),
            pltpu.VMEM((WIDE * SIDE, 4 * SIDE), bf16),
            pltpu.VMEM((WIDE * SIDE, 4 * SIDE), bf16),
            pltpu.VMEM((4 * SIDE, WIDE * SIDE), bf16),
            pltpu.SemaphoreType.DMA((own // WIDE // groups,)),
            pltpu.SemaphoreType.DMA((6,)),
            pltpu.SemaphoreType.DMA((own // WIDE // groups,)),
        ],
        compiler_params=streaming,
        name="mix",
    )(message, weights, *known)
    message = lax.all_to_all(message, "seq", 0, 0)

    return pl.pallas_call(
        join_kernel,
        in_specs=[whole] * 6,
        out_specs=hbm,
        out_shape=jax.ShapeDtypeStruct((rows, channels), bf16),
        scratch_shapes=[
            pltpu.VMEM((rows, channels), bf16),
            pltpu.VMEM((1, channels), f32),
            pltpu.VMEM((8, channels), f32),
            pltpu.SemaphoreType.DMA((steps,)),
        ],
        compiler_params=resident,
        name="join",
    )(message, q_short, skipped, ends, short_weight, skip_bias[None])


def solution(mesh):
    in_specs = (
        P("seq", "ch"),
        P("seq", "ch"),
        P("seq", "ch"),
        P(None, None, "ch"),
        P("ch"),
        P("ch", "seq"),
    )
    out_specs = P("seq", "ch")
    return jax.shard_map(shards, mesh=mesh, in_specs=in_specs, out_specs=out_specs, check_vma=False)
```

profile of v0, /device:TPU:1, one launch (start us, length us, event | category | flops | bytes accessed | tf_op | source)
XLA Modules:
  0.0 72.1 jit_solution(570179062636870882)
XLA Ops:
  0.0 0.0 copy-start.2
  0.0 6.4 %gate.1 = bf16[32,144,128]{2,1,0:T(8,128)(2,1)} custom-call(bf16[512,1024]{1,0:T(8,128)(2,1)} %q_ref, bf16[512,1024]{1,0:T(8,128)(2,1)} %k_ref, bf16[512,1024]{1,0:T(8,128)(2,1)} %v_ref, f32[3,3,1024]{2,1,0:T(4,128)} %w_ref.1, f32[64,512]{1,0:T(8,128)} %taps_hbm.1), custom_call_target="tpu_custom_call" | custom-call | tf_op jit(solution)/shard_map/gate/pallas_call | solution.py:607
  6.5 0.0 copy-start.7
  6.5 0.0 copy-start
  6.5 0.0 copy-start.1
  6.5 0.0 copy-start.8
  6.5 8.8 %all-to-all-start = ((bf16[32,144,128]{2,1,0:T(8,128)(2,1)}), bf16[32,144,128]{2,1,0:T(8,128)(2,1)}, u32[]{:S(2)}, u32[]{:S(2)}) async-start(bf16[32,144,128]{2,1,0:T(8,128)(2,1)} %gate.1), calls=%async_computation | async-start | bytes 2359296 | tf_op jit(solution)/shard_map/all_to_all | solution.py:632
  15.3 0.0 copy-done.7
  15.3 0.1 constant_dynamic-slice_fusion
  15.4 0.6 pad.4.w_hbm
  16.0 0.0 copy-done.2
  16.0 0.0 copy-done
  16.0 0.0 copy-done.1
  16.0 0.0 copy-done.8
  16.0 2.3 %local.1 = (f32[512,1024]{1,0:T(8,128)S(1)}, f32[512,1024]{1,0:T(8,128)S(1)}, f32[8,1024]{1,0:T(8,128)S(1)}) custom-call(bf16[512,1024]{1,0:T(8,128)(2,1)S(1)} %copy-done, bf16[512,1024]{1,0:T(8,128)(2,1)S(1)} %copy-done.1, bf16[512,1024]{1,0:T(8,128)(2,1)S(1)} %copy-done.2, f32[3,3,1024]{2,1,0:T(4,128)S(1)} %copy-done.7, f32[1,1024]{1,0:T(1,128)S(1)} %bitcast.1), custom_call_target="tpu_custom_call" | custom-call | flops 10485760 | bytes 7340032 | tf_op jit(solution)/shard_map/local/pallas_call | solution.py:634
  18.3 0.0 copy-start.3
  18.3 1.3 %copy-done.3 = f32[512,1024]{1,0:T(8,128)} copy-done((f32[512,1024]{1,0:T(8,128)}, f32[512,1024]{1,0:T(8,128)S(1)}, u32[]{:S(2)}) %copy-start.3) | copy-done | bytes 2097176
  19.6 0.0 copy-start.5
  19.6 1.3 %copy-done.5 = f32[512,1024]{1,0:T(8,128)} copy-done((f32[512,1024]{1,0:T(8,128)}, f32[512,1024]{1,0:T(8,128)S(1)}, u32[]{:S(2)}) %copy-start.5) | copy-done | bytes 2097176
  20.9 12.8 %all-to-all-done.in_hbm = bf16[32,144,128]{2,1,0:T(8,128)(2,1)} async-done(((bf16[32,144,128]{2,1,0:T(8,128)(2,1)}), bf16[32,144,128]{2,1,0:T(8,128)(2,1)}, u32[]{:S(2)}, u32[]{:S(2)}) %all-to-all-start) | async-done | bytes 1179680 | tf_op jit(solution)/shard_map/all_to_all | solution.py:632
  33.7 0.0 copy-start.6
  33.7 12.5 %mix.1 = bf16[32,136,128]{2,1,0:T(8,128)(2,1)} custom-call(bf16[32,144,128]{2,1,0:T(8,128)(2,1)} %all-to-all-done.in_hbm, f32[3,3,128]{2,1,0:T(4,128)} %pad.4.w_hbm, bf16[512,256]{1,0:T(8,128)(2,1)} %constant.24.clone.first_hbm, bf16[768,256]{1,0:T(8,128)(2,1)} %constant.25.clone.second_hbm, bf16[768,256]{1,0:T(8,128)(2,1)} %constant.26.clone.third_hbm, ...), custom_call_target="tpu_custom_call" | custom-call | tf_op jit(solution)/shard_map/mix/pallas_call | solution.py:657
  46.2 0.0 copy-start.4
  46.2 22.5 %all_to_all.10.in_ref = bf16[32,136,128]{2,1,0:T(8,128)(2,1)S(1)} all-to-all(bf16[32,136,128]{2,1,0:T(8,128)(2,1)} %mix.1), channel_id=1, replica_groups=mesh['seq'=32,'ch'=8] {'seq'}, dimensions={0} | all-to-all | bytes 2228224 | tf_op jit(solution)/shard_map/all_to_all | solution.py:686
  68.7 0.0 copy-done.6
  68.7 0.0 copy-done.4
  68.7 3.4 %join.1 = bf16[512,1024]{1,0:T(8,128)(2,1)} custom-call(bf16[32,136,128]{2,1,0:T(8,128)(2,1)S(1)} %all_to_all.10.in_ref, f32[512,1024]{1,0:T(8,128)S(1)} %copy-done.4, f32[512,1024]{1,0:T(8,128)S(1)} %copy-done.6, f32[8,1024]{1,0:T(8,128)S(1)} %get-tuple-element.42.ends_ref, f32[3,3,1024]{2,1,0:T(4,128)S(1)} %copy-done.7, f32[1,1024]{1,0:T(1,128)S(1)} %bitcast.2), custom_call_target="tpu_custom_call" | custom-call | tf_op jit(solution)/shard_map/join/pallas_call | solution.py:688
Async XLA Ops:
  0.0 16.0 %copy-start.2 = (bf16[512,1024]{1,0:T(8,128)(2,1)S(1)}, bf16[512,1024]{1,0:T(8,128)(2,1)}, u32[]{:S(2)}) copy-start(bf16[512,1024]{1,0:T(8,128)(2,1)} %v_ref) | copy-start | bytes 3145732
  6.5 8.8 %copy-start.7 = (f32[3,3,1024]{2,1,0:T(4,128)S(1)}, f32[3,3,1024]{2,1,0:T(4,128)}, u32[]{:S(2)}) copy-start(f32[3,3,1024]{2,1,0:T(4,128)} %w_ref.1) | copy-start | bytes 110596
  6.5 9.5 %copy-start = (bf16[512,1024]{1,0:T(8,128)(2,1)S(1)}, bf16[512,1024]{1,0:T(8,128)(2,1)}, u32[]{:S(2)}) copy-start(bf16[512,1024]{1,0:T(8,128)(2,1)} %q_ref) | copy-start | bytes 3145732
  6.5 9.5 %copy-start.1 = (bf16[512,1024]{1,0:T(8,128)(2,1)S(1)}, bf16[512,1024]{1,0:T(8,128)(2,1)}, u32[]{:S(2)}) copy-start(bf16[512,1024]{1,0:T(8,128)(2,1)} %k_ref) | copy-start | bytes 3145732
  6.5 9.5 %copy-start.8 = (f32[1024]{0:T(1024)S(1)}, f32[1024]{0:T(1024)}, u32[]{:S(2)}) copy-start(f32[1024]{0:T(1024)} %param.15) | copy-start | bytes 12292
  6.5 27.2 %all-to-all-start = ((bf16[32,144,128]{2,1,0:T(8,128)(2,1)}), bf16[32,144,128]{2,1,0:T(8,128)(2,1)}, u32[]{:S(2)}, u32[]{:S(2)}) async-start(bf16[32,144,128]{2,1,0:T(8,128)(2,1)} %gate.1), calls=%async_computation | async-start | bytes 2359296 | tf_op jit(solution)/shard_map/all_to_all | solution.py:632
  18.3 1.3 %copy-start.3 = (f32[512,1024]{1,0:T(8,128)}, f32[512,1024]{1,0:T(8,128)S(1)}, u32[]{:S(2)}) copy-start(f32[512,1024]{1,0:T(8,128)S(1)} %get-tuple-element.40.q_ref) | copy-start | bytes 6291460
  19.6 1.3 %copy-start.5 = (f32[512,1024]{1,0:T(8,128)}, f32[512,1024]{1,0:T(8,128)S(1)}, u32[]{:S(2)}) copy-start(f32[512,1024]{1,0:T(8,128)S(1)} %get-tuple-element.41.s_ref) | copy-start | bytes 6291460
  33.7 35.0 %copy-start.6 = (f32[512,1024]{1,0:T(8,128)S(1)}, f32[512,1024]{1,0:T(8,128)}, u32[]{:S(2)}) copy-start(f32[512,1024]{1,0:T(8,128)} %copy-done.5) | copy-start | bytes 6291460
  46.2 22.5 %copy-start.4 = (f32[512,1024]{1,0:T(8,128)S(1)}, f32[512,1024]{1,0:T(8,128)}, u32[]{:S(2)}) copy-start(f32[512,1024]{1,0:T(8,128)} %copy-done.3) | copy-start | bytes 6291460
where the time goes:
time: 72.4 us; the launch traced here: 72.1 us
  Pallas kernels  24.6 us (34%)
  blocking collectives  22.5 us (31%)
  waiting for transfers between devices  12.8 us (18%)
  starting transfers between devices  8.78 us (12%)
  local copies, waits for them, and re-layouts  3.35 us (5%)
    all_to_all x1, blocking collectives, shards(): message = lax.all_to_all(message, 'seq', 0, 0)  22.5 us
    all_to_all x1, waiting for transfers between devices, shards(): message = lax.all_to_all(message, 'seq', 0, 0)  12.8 us
    pallas_call x1, Pallas kernels, shards(): pl.pallas_call(mix_kernel, in_specs=[hbm] * 7, out_specs=hbm, out_shape=j...  12.5 us
    all_to_all x1, starting transfers between devices, shards(): message = lax.all_to_all(message, 'seq', 0, 0)  8.78 us
    pallas_call x1, Pallas kernels, shards(): pl.pallas_call(gate_kernel, in_specs=[hbm] * 5, out_specs=hbm, out_shape=...  6.44 us
    pallas_call x1, Pallas kernels, shards(): pl.pallas_call(join_kernel, in_specs=[whole] * 6, out_specs=hbm, out_shap...  3.37 us
    unnamed x18, local copies, waits for them, and re-layouts  2.68 us
    pallas_call x1, Pallas kernels, shards(): pl.pallas_call(local_kernel, in_specs=[whole] * 5, out_specs=[whole] * 3,...  2.27 us
  transfers between devices with their start and end apart: 1, of which 1 were waited for; matrix products, arithmetic and copies ran while one was open for 1% of the time, Pallas kernels for 3%

commit v1 on v0

--- a/solution.py
+++ b/solution.py
@@ -11,10 +11,11 @@
 GROUP_SIZE = 16
 SIDE = 128
 LANES = 128
+LAGS = 6
 WIDE = 4
-CODE_SPAN = 240.0
-CODE_TOP = 4096.0
-CODE_GAIN = CODE_SPAN / math.log2(1.0 + CODE_TOP)
+CODE_POWER = 17
+CODE_TOP = 2.0 ** (120.0 / CODE_POWER)
+CODE_LEAST = 2.0**-126
 INV_LN2 = 1.0 / math.log(2.0)
 RESIDENT_LIMIT = 12 * 1024 * 1024
 STREAMING_LIMIT = 60 * 1024 * 1024
@@ -23,46 +24,34 @@
 
 
 def encode(value, to_units):
-    level = jnp.log(1.0 + jnp.abs(value) * to_units) * (CODE_GAIN * INV_LN2)
-    code = jnp.exp2(level - CODE_SPAN / 2)
-    return jnp.where(value < 0, -code, code)
+    unit = value * to_units
+    square = unit * unit
+    fourth = square * square
+    eighth = fourth * fourth
+    return unit * (eighth * eighth)
 
 
 def decode(code, from_units):
-    level = jnp.log(jnp.abs(code)) * (INV_LN2 / CODE_GAIN)
-    size = (jnp.exp2(level + CODE_SPAN / 2 / CODE_GAIN) - 1.0) * from_units
-    return jnp.where(code < 0, -size, size)
+    size = jnp.maximum(jnp.abs(code), CODE_LEAST)
+    root = jnp.exp2(jnp.log(size) * (INV_LN2 * (1.0 / CODE_POWER - 1.0)))
+    return code * root * from_units
 
 
 def code_scale(largest):
     return (jnp.maximum(largest, 1e-30) * 1.01).astype(bf16).astype(f32)
 
 
-def tables():
+def table_blocks():
     side = np.arange(SIDE)
     inner = 2 * np.pi / SIDE * (side[:, None] * side[None, :] % SIDE)
     outer = 2 * np.pi / (4 * SIDE) * (side[None, :] * (4 * side[:, None] + 1) % (4 * SIDE))
     twist = 2 * np.pi / (4 * SIDE * SIDE) * (side[None, :] * (4 * side[:, None] + 1))
-    first = np.concatenate([np.cos(outer), -np.sin(outer)], axis=0)
-    second = np.block([[np.cos(inner), -np.sin(inner)], [np.sin(inner), np.cos(inner)]])
-    third = np.block([[np.cos(inner), np.sin(inner)], [-np.sin(inner), np.cos(inner)]])
-    fourth = np.concatenate([np.cos(outer).T, -np.sin(outer).T], axis=1)
-
-    def parts(table):
-        high = table.astype(jnp.bfloat16)
-        return high, (table - high.astype(np.float64)).astype(jnp.bfloat16)
-
-    def beside(table):
-        high, low = parts(table)
-        return np.concatenate([high, high, low], axis=0)
-
-    return (
-        np.concatenate([np.concatenate([part, part], axis=1) for part in parts(first)], axis=0),
-        beside(second),
-        beside(third),
-        np.concatenate(parts(fourth), axis=0),
-        np.stack([np.cos(twist), np.sin(twist)]).astype(np.float32),
-    )
+    blocks = []
+    for angle in (inner, outer, outer.T, twist):
+        for table in (np.cos(angle), np.sin(angle)):
+            high = table.astype(jnp.bfloat16)
+            blocks += [high, (table - high.astype(np.float64)).astype(jnp.bfloat16)]
+    return np.concatenate(blocks, axis=0)
 
 
 def dot(left, right):
@@ -139,9 +128,12 @@
     for step in range(steps):
         for at in range(2):
             stream_copy(at, step).wait()
-
-        def tile(block, slot, step=step):
-            lanes = pl.ds(pl.multiple_of(block * LANES, LANES), LANES)
+        if step == steps - 1:
+            taps_copy.wait()
+            q_copy.wait()
+
+        def tile(block, step=step):
+            lanes = slice(block * LANES, (block + 1) * LANES)
             shorts = []
             for at, buf in enumerate((k_buf, v_buf)):
                 if step == 0:
@@ -150,35 +142,27 @@
                     before = buf[step * SIDE - 16 : step * SIDE, lanes].astype(f32)[8:]
                 shorts.append(
                     short_conv(
-                        buf, step * SIDE, lanes, before, w_buf[1 + at, :, lanes], pads.at[slot, at]
+                        buf, step * SIDE, lanes, before, w_buf[1 + at, :, lanes], pads.at[block, at]
                     )
                 )
             gated = shorts[0] * shorts[1]
             scale = code_scale(jnp.max(jnp.abs(gated), axis=0, keepdims=True))
             scales[step : step + 1, lanes] = scale
             code = encode(gated, CODE_TOP / scale).T.astype(bf16)
-            first = pl.multiple_of(block * dests, dests)
-            out_ref[pl.ds(first, dests), step * per : (step + 1) * per, :] = code.reshape(
-                dests, per, LANES
-            )
-
-        def tiles(n, carry):
-            tile(2 * n, 0)
-            tile(2 * n + 1, 1)
-            return carry
-
-        lax.fori_loop(0, blocks // 2, tiles, 0)
+            span = slice(block * dests, (block + 1) * dests)
+            out_ref[span, step * per : (step + 1) * per, :] = code.reshape(dests, per, LANES)
+
+        for block in range(blocks):
+            tile(block)
         if step < steps - 1:
             out_copy(step).start()
 
-    taps_copy.wait()
-    q_copy.wait()
-
-    def tail(block, slot):
-        lanes = pl.ds(pl.multiple_of(block * LANES, LANES), LANES)
+    def tail(block):
+        slot = block
+        lanes = slice(block * LANES, (block + 1) * LANES)
         for a in range(steps):
             taps_in[slot, a * held : (a + 1) * held, :] = taps_buf[
-                pl.ds(pl.multiple_of(block * held, held), held), a * LANES : (a + 1) * LANES
+                block * held : (block + 1) * held, a * LANES : (a + 1) * LANES
             ]
         taps_at = steps * held
         for a in range(steps):
@@ -204,35 +188,20 @@
             both = jnp.concatenate([taps_code[8 * d : 8 * d + 8], last], axis=0).astype(bf16)
             out_ref[block * dests + d, base : base + 16, :] = both
 
-    def tails(n, carry):
-        tail(2 * n, 0)
-        tail(2 * n + 1, 1)
-        return carry
-
     scales[steps:, :] = jnp.zeros((8 - steps, channels), f32)
     q_ends[...] = jnp.zeros_like(q_ends)
-    lax.fori_loop(0, blocks // 2, tails, 0)
+    for block in range(blocks):
+        tail(block)
     out_copy(steps - 1).start()
     for step in range(steps):
         out_copy(step).wait()
 
 
 def mix_kernel(
-    in_hbm,
-    w_hbm,
-    first_hbm,
-    second_hbm,
-    third_hbm,
-    fourth_hbm,
-    twist_hbm,
-    out_hbm,
     in_ref,
     w_ref,
-    first,
-    second,
-    third,
-    fourth,
-    twist,
+    table_ref,
+    out_hbm,
     out_ref,
     signal_0,
     signal_1,
@@ -240,7 +209,6 @@
     result_1,
     taps,
     spectra,
-    largest,
     units,
     tails,
     back_tails,
@@ -249,8 +217,13 @@
     turned,
     filtered,
     unturned,
-    in_sems,
-    table_sems,
+    first_raw,
+    third_raw,
+    first,
+    second,
+    third,
+    fourth,
+    twist,
     out_sems,
 ):
     signals, results = (signal_0, signal_1), (result_0, result_1)
@@ -263,52 +236,43 @@
     slots = count // groups
     slot_blocks = blocks // slots
 
-    def in_copy(slot):
-        span = pl.ds(slot * slot_blocks, slot_blocks)
-        return pltpu.make_async_copy(in_hbm.at[span], in_ref.at[span], in_sems.at[slot])
-
     def out_copy(slot):
         span = pl.ds(slot * slot_blocks, slot_blocks)
         return pltpu.make_async_copy(out_ref.at[span], out_hbm.at[span], out_sems.at[slot])
 
-    table_copies = [
-        pltpu.make_async_copy(source, target, table_sems.at[at])
-        for at, (source, target) in enumerate(
-            (
-                (w_hbm, w_ref),
-                (twist_hbm, twist),
-                (first_hbm, first),
-                (second_hbm, second),
-                (third_hbm, third),
-                (fourth_hbm, fourth),
-            )
-        )
-    ]
-    for slot in range(slots):
-        in_copy(slot).start()
-    for copy in table_copies:
-        copy.start()
-
-    lane = lax.broadcasted_iota(jnp.int32, (GROUP_SIZE, LANES), 1)
-
-    def start_of(j, group):
-        return starts[j * channels + group * GROUP_SIZE : j * channels + (group + 1) * GROUP_SIZE, :]
-
-    def unpack(slot, group, with_starts):
+    def unpack(slot, group):
         for i in range(slot_blocks):
             j = slot * slot_blocks + i
             for a in range(per_block):
                 at = a * channels + group * GROUP_SIZE
-                value = decode(in_ref[j, at : at + GROUP_SIZE, :].astype(f32), 1.0)
-                if a == 0 and with_starts:
-                    value = jnp.where(lane < 2, start_of(j, group), value)
                 place = (j * per_block + a) * GROUP_SIZE
-                signals[group][place : place + GROUP_SIZE, :] = value
+                code = in_ref[j, at : at + GROUP_SIZE, :].astype(f32)
+                signals[group][place : place + GROUP_SIZE, :] = code
 
     for slot in range(slots):
-        in_copy(slot).wait()
-        unpack(slot, 0, False)
-    table_copies[0].wait()
+        unpack(slot, 0)
+
+    def block(at):
+        return table_ref[at * SIDE : (at + 1) * SIDE, :]
+
+    for part in range(2):
+        inner_cos, inner_sin = block(part), block(2 + part)
+        for at in ((0, 2 * SIDE), (4 * SIDE,))[part]:
+            second[at : at + SIDE, :SIDE] = inner_cos
+            second[at : at + SIDE, SIDE:] = -inner_sin
+            second[at + SIDE : at + 2 * SIDE, :SIDE] = inner_sin
+            second[at + SIDE : at + 2 * SIDE, SIDE:] = inner_cos
+            third[at : at + SIDE, :SIDE] = inner_cos
+            third[at : at + SIDE, SIDE:] = inner_sin
+            third[at + SIDE : at + 2 * SIDE, :SIDE] = -inner_sin
+            third[at + SIDE : at + 2 * SIDE, SIDE:] = inner_cos
+        at = 2 * part * SIDE
+        for span in (slice(0, SIDE), slice(SIDE, 2 * SIDE)):
+            first[at : at + SIDE, span] = block(4 + part)
+            first[at + SIDE : at + 2 * SIDE, span] = -block(6 + part)
+        fourth[part * SIDE : (part + 1) * SIDE, :SIDE] = block(8 + part)
+        fourth[part * SIDE : (part + 1) * SIDE, SIDE:] = -block(10 + part)
+        twist[part] = block(12 + 2 * part).astype(f32) + block(13 + 2 * part).astype(f32)
 
     of_message = in_ref[:, data : data + 16, :].astype(f32)
     tails[...] = of_message[:, 8:].reshape(blocks * 8, LANES)
@@ -319,7 +283,6 @@
 
     def gated_starts():
         block = lax.broadcasted_iota(jnp.int32, (blocks, LANES), 0)
-        lanes = lax.broadcasted_iota(jnp.int32, (blocks, LANES), 1)
         shorts = []
         for at in range(2):
             ago_2, ago_1, now, later = [
@@ -340,30 +303,12 @@
             asked = pltpu.roll(tails[pl.ds(at, blocks, stride=8), :], LANES - 3 * channels, 1)
             asked = jnp.where(block == 0, 0.0, pltpu.roll(asked, 1, 0))
             back_tails[pl.ds(1 + at, blocks, stride=8), :] = asked
-        level = pltpu.roll(tails[pl.ds(0, blocks, stride=8), :], LANES - channels, 1)
-        to_level = CODE_TOP / jnp.where(lanes < channels, level, 1.0)
-        packed = jnp.zeros((blocks, LANES), f32)
+        packed = [shorts[0][token] * shorts[1][token] for token in range(2)]
         for token in range(2):
-            parts = halves(shorts[0][token] * shorts[1][token] * to_level)
-            for at, part in enumerate(parts):
-                place = 2 * token + at
-                moved = pltpu.roll(part.astype(f32), place * channels, 1)
-                packed = jnp.where(lanes // channels == place, moved, packed)
-        lane = lax.broadcasted_iota(jnp.int32, (blocks, channels, LANES), 2)
-        row = lax.broadcasted_iota(jnp.int32, (blocks, channels, LANES), 1)
-        picked = jnp.where(lane % channels == row, packed[:, None, :], 0.0).astype(bf16)
-        from_lane = lax.broadcasted_iota(jnp.int32, (LANES, LANES), 0)
-        to_lane = lax.broadcasted_iota(jnp.int32, (LANES, LANES), 1)
-        place = jnp.where(from_lane // (2 * channels) == to_lane, 1.0, 0.0).astype(bf16)
-        starts[...] = dot(picked.reshape(blocks * channels, LANES), place)
+            starts[token] = jnp.zeros((SIDE, LANES), f32)
+            starts[token, pl.ds(0, blocks, stride=per_block), :] = packed[token]
 
     gated_starts()
-    for j in range(blocks):
-        place = j * per_block * GROUP_SIZE
-        span = slice(place, place + GROUP_SIZE)
-        signal_0[span, :] = jnp.where(lane < 2, start_of(j, 0), signal_0[span, :])
-    for copy in table_copies[1:]:
-        copy.wait()
 
     cos, sin = twist[0], twist[1]
 
@@ -376,30 +321,38 @@
         rows = used * SIDE
         return dot(ref[:rows], table[: 4 * SIDE]) + dot(ref[:rows, : 2 * SIDE], table[4 * SIDE :])
 
+    lane = lax.broadcasted_iota(jnp.int32, (SIDE, LANES), 1)
+    starts_block = lax.broadcasted_iota(jnp.int32, (SIDE, LANES), 0) % per_block == 0
+    start_masks = [starts_block & (lane == token) for token in range(2)]
+
+    def load(n, group):
+        level = pltpu.roll(levels[...], LANES - channels - WIDE * n, 1) * (1.0 / CODE_TOP)
+        first_tokens = [pltpu.roll(starts[token], LANES - WIDE * n, 1) for token in range(2)]
+        at = WIDE * (n - group * slots)
+        values = []
+        for i in range(WIDE):
+            code = signals[group][pl.ds(at + i, SIDE, stride=GROUP_SIZE), :]
+            value = decode(code, level[:, i : i + 1])
+            for token in range(2):
+                value = jnp.where(start_masks[token], first_tokens[token][:, i : i + 1], value)
+            values.append(value)
+        return values
+
     def first_side(values):
         for pair in range(len(values) // 2):
             high, low = halves(jnp.concatenate(values[2 * pair : 2 * pair + 2], axis=1))
             wide = dot(first[...], jnp.concatenate([high, low], axis=0))
-            wide = wide[: 2 * SIDE] + wide[2 * SIDE :]
-            for at in range(2):
-                re = wide[:SIDE, at * SIDE : (at + 1) * SIDE]
-                im = wide[SIDE:, at * SIDE : (at + 1) * SIDE]
-                store_halves(
-                    turned,
-                    2 * pair + at,
-                    jnp.concatenate([re * cos + im * sin, im * cos - re * sin], axis=1),
-                )
-
-    def load(n, group):
-        level = pltpu.roll(levels[...], LANES - channels - WIDE * n, 1) * (1.0 / CODE_TOP)
-        at = WIDE * (n - group * slots)
-        return [
-            signals[group][pl.ds(at + i, SIDE, stride=GROUP_SIZE), :] * level[:, i : i + 1]
-            for i in range(WIDE)
-        ]
-
-    def second_side(n):
-        spectrum = table_right(turned, second)
+            first_raw[pair] = wide[: 2 * SIDE] + wide[2 * SIDE :]
+
+    def turn(used=WIDE):
+        for at in range(used):
+            span = slice(at % 2 * SIDE, (at % 2 + 1) * SIDE)
+            re, im = first_raw[at // 2, :SIDE, span], first_raw[at // 2, SIDE:, span]
+            store_halves(
+                turned, at, jnp.concatenate([re * cos + im * sin, im * cos - re * sin], axis=1)
+            )
+
+    def filter_spectrum(n, spectrum):
         of_taps = spectra[WIDE * n // GROUP_SIZE]
         f_re, f_im = of_taps[:, :SIDE], of_taps[:, SIDE:]
         for at in range(WIDE):
@@ -411,85 +364,81 @@
                 jnp.concatenate([s_re * f_re - s_im * f_im, s_re * f_im + s_im * f_re], axis=1),
             )
 
-    def second_side_back():
-        back = table_right(filtered, third)
+    def turn_back():
         for at in range(WIDE):
-            re = back[at * SIDE : (at + 1) * SIDE, :SIDE]
-            im = back[at * SIDE : (at + 1) * SIDE, SIDE:]
+            re = third_raw[at * SIDE : (at + 1) * SIDE, :SIDE]
+            im = third_raw[at * SIDE : (at + 1) * SIDE, SIDE:]
             high, low = halves(jnp.concatenate([re * cos - im * sin, im * cos + re * sin], axis=0))
             unturned[: 2 * SIDE, at * SIDE : (at + 1) * SIDE] = high
             unturned[2 * SIDE :, at * SIDE : (at + 1) * SIDE] = low
 
-    def first_side_back(n, group):
+    def first_side_back():
+        found = []
         for pair in range(WIDE // 2):
             span = slice(2 * pair * SIDE, (2 * pair + 2) * SIDE)
             done = dot(fourth[...], unturned[: 2 * SIDE, span])
-            done = done[:SIDE] + done[SIDE:] + dot(fourth[:SIDE], unturned[2 * SIDE :, span])
-            top = jnp.max(jnp.abs(done), axis=0, keepdims=True)
-            for i in range(2):
-                span = slice(i * SIDE, (i + 1) * SIDE)
-                at = WIDE * n + 2 * pair + i
-                place = pl.ds(at - group * GROUP_SIZE, SIDE, stride=GROUP_SIZE)
-                results[group][place, :] = done[:, span]
-                largest[pl.ds(at, 1), :] = top[:, span]
-
-    def scale_group(group):
-        span = slice(group * GROUP_SIZE, (group + 1) * GROUP_SIZE)
-        scale = code_scale(jnp.max(largest[span, :], axis=1, keepdims=True))
-        units[span, :] = jnp.broadcast_to(scale, (GROUP_SIZE, LANES))
+            found.append(
+                done[:SIDE] + done[SIDE:] + dot(fourth[:SIDE], unturned[2 * SIDE :, span])
+            )
+        return found
+
+    def finish(n, group, found):
+        for i in range(WIDE):
+            value = found[i // 2][:, i % 2 * SIDE : (i % 2 + 1) * SIDE]
+            top = jnp.max(jnp.max(jnp.abs(value), axis=0, keepdims=True), axis=1, keepdims=True)
+            scale = code_scale(top)
+            channel = WIDE * n + i
+            units[pl.ds(channel, 1), :] = jnp.broadcast_to(scale, (1, LANES))
+            place = pl.ds(channel - group * GROUP_SIZE, SIDE, stride=GROUP_SIZE)
+            results[group][place, :] = encode(value, CODE_TOP / scale)
+
+    def step(n, load_group, finish_group, active=(True,) * LAGS):
+        loads, turns, filters, filtered_back, turns_back, finishes = active
+        if filters:
+            spectrum = table_right(turned, second)
+        if finishes:
+            found = first_side_back()
+        if turns:
+            turn()
+        if turns_back:
+            turn_back()
+        if filtered_back:
+            third_raw[...] = table_right(filtered, third)
+        if loads:
+            first_side(load(n, load_group))
+        if finishes:
+            finish(n - 5, finish_group, found)
+        if filters:
+            filter_spectrum(n - 2, spectrum)
 
     def pack(slot, group):
-        to_units = CODE_TOP / units[group * GROUP_SIZE : (group + 1) * GROUP_SIZE, :]
         for i in range(slot_blocks):
             j = slot * slot_blocks + i
             for a in range(per_block):
                 at = a * channels + group * GROUP_SIZE
                 place = (j * per_block + a) * GROUP_SIZE
-                value = results[group][place : place + GROUP_SIZE, :]
-                out_ref[j, at : at + GROUP_SIZE, :] = encode(value, to_units).astype(bf16)
-
-    def step(n, carry):
-        first_side_back(n - 3, 0)
-        second_side_back()
-        second_side(n - 1)
-        first_side(load(n, 1))
-        return carry
+                code = results[group][place : place + GROUP_SIZE, :]
+                out_ref[j, at : at + GROUP_SIZE, :] = code.astype(bf16)
 
     first_side([taps[pl.ds(g, SIDE, stride=groups), :] for g in range(groups)])
+    turn(groups)
     spectra[...] = table_right(turned, second, groups).reshape(groups, SIDE, 2 * SIDE) * (
         1.0 / (SIDE * SIDE)
     )
-    first_side(load(0, 0))
-    unpack(0, 1, True)
-    second_side(0)
-    first_side(load(1, 0))
-    unpack(1, 1, True)
-    second_side_back()
-    second_side(1)
-    first_side(load(2, 0))
-    unpack(2, 1, True)
-    first_side_back(0, 0)
-    second_side_back()
-    second_side(2)
-    first_side(load(3, 0))
-    unpack(3, 1, True)
-    lax.fori_loop(4, 7, step, 0)
-    scale_group(0)
-    pack(0, 0)
-    first_side_back(4, 1)
-    second_side_back()
-    second_side(6)
-    first_side(load(7, 1))
-    pack(1, 0)
-    first_side_back(5, 1)
-    second_side_back()
-    second_side(7)
-    pack(2, 0)
-    first_side_back(6, 1)
-    second_side_back()
-    pack(3, 0)
-    first_side_back(7, 1)
-    scale_group(1)
+    for n in range(slots):
+        step(n, 0, 0, tuple(n >= lag for lag in range(LAGS)))
+        unpack(n, 1)
+    step(slots, 1, 0, tuple(slots >= lag for lag in range(LAGS)))
+
+    def steady(n, carry):
+        step(n, 1, 0)
+        return carry
+
+    lax.fori_loop(slots + 1, count, steady, 0)
+    for n in range(count, count + LAGS - 1):
+        step(n, 1, int(n - LAGS + 1 >= slots), tuple(n - lag < count for lag in range(LAGS)))
+        if n > count:
+            pack(n - count - 1, 0)
 
     diagonal = lax.broadcasted_iota(jnp.int32, (channels, LANES), 1) == lax.broadcasted_iota(
         jnp.int32, (channels, LANES), 0
@@ -565,10 +514,10 @@
     for step in range(steps):
         span = slice(step * SIDE, (step + 1) * SIDE)
 
-        def column(block, carry, step=step, span=span):
-            lanes = pl.ds(pl.multiple_of(block * LANES, LANES), LANES)
-            first = pl.multiple_of(block * sources, sources)
-            code = in_ref[pl.ds(first, sources), step * per : (step + 1) * per, :]
+        for block in range(blocks):
+            lanes = slice(block * LANES, (block + 1) * LANES)
+            of_block = slice(block * sources, (block + 1) * sources)
+            code = in_ref[of_block, step * per : (step + 1) * per, :]
             tile = code.astype(f32).reshape(LANES, SIDE).T
             long_conv = decode(tile, units[:, lanes])
             q_short, skipped = q_ref[span, lanes], s_ref[span, lanes]
@@ -579,9 +528,6 @@
                 q_short = jnp.concatenate([q_start, q_short[8:]], axis=0)
                 skipped = jnp.concatenate([s_start, skipped[8:]], axis=0)
             out_buf[span, lanes] = (q_short * (long_conv + skipped)).astype(bf16)
-            return carry
-
-        lax.fori_loop(0, blocks, column, 0, unroll=2)
         rows_at = pl.ds(step * SIDE, SIDE)
         copies.append(
             pltpu.make_async_copy(out_buf.at[rows_at], out_hbm.at[rows_at], sems.at[step])
@@ -616,18 +562,18 @@
             pltpu.VMEM(short_weight.shape, f32),
             pltpu.VMEM(filter_taps.shape, f32),
             pltpu.VMEM((seq, sent + 16, LANES), bf16),
-            pltpu.VMEM((2, 2, 16 + SIDE, LANES), f32),
+            pltpu.VMEM((blocks, 2, 16 + SIDE, LANES), f32),
             pltpu.VMEM((8, channels), f32),
-            pltpu.VMEM((2, 8, LANES), f32),
-            pltpu.VMEM((2, 8, LANES), f32),
-            pltpu.VMEM((2, 2 * steps * filter_taps.shape[0] // blocks, LANES), f32),
+            pltpu.VMEM((blocks, 8, LANES), f32),
+            pltpu.VMEM((blocks, 8, LANES), f32),
+            pltpu.VMEM((blocks, 2 * steps * filter_taps.shape[0] // blocks, LANES), f32),
             pltpu.SemaphoreType.DMA((4, steps)),
         ],
         compiler_params=streaming,
         name="gate",
     )(query_in, key_in, value_in, short_weight, filter_taps)
-    message, query_in, key_in, value_in, short_weight, skip_bias, *known = lax.optimization_barrier(
-        (message, query_in, key_in, value_in, short_weight, skip_bias, *tables())
+    message, query_in, key_in, value_in, short_weight, skip_bias, known = lax.optimization_barrier(
+        (message, query_in, key_in, value_in, short_weight, skip_bias, table_blocks())
     )
     message = lax.all_to_all(message, "seq", 0, 0)
 
@@ -653,36 +599,36 @@
         (message, q_short, skipped, ends, weights)
     )
 
-    table_shapes = [pltpu.VMEM(table.shape, table.dtype) for table in known]
     message = pl.pallas_call(
         mix_kernel,
-        in_specs=[hbm] * 7,
+        in_specs=[whole] * 3,
         out_specs=hbm,
         out_shape=jax.ShapeDtypeStruct((seq, sent + 8, LANES), bf16),
         scratch_shapes=[
-            pltpu.VMEM((seq, sent + 16, LANES), bf16),
-            pltpu.VMEM(weights.shape, f32),
-            *table_shapes,
             pltpu.VMEM((seq, sent + 8, LANES), bf16),
             *[pltpu.VMEM((seq * sent // groups, LANES), f32)] * (2 * groups),
             pltpu.VMEM((seq * 8, LANES), f32),
             pltpu.VMEM((groups, SIDE, 2 * SIDE), f32),
             pltpu.VMEM((own, LANES), f32),
-            pltpu.VMEM((own, LANES), f32),
             pltpu.VMEM((seq * 8, LANES), f32),
             pltpu.VMEM((seq * 8, LANES), f32),
             pltpu.VMEM((SIDE, LANES), f32),
-            pltpu.VMEM((seq * own, LANES), f32),
+            pltpu.VMEM((2, SIDE, LANES), f32),
             pltpu.VMEM((WIDE * SIDE, 4 * SIDE), bf16),
             pltpu.VMEM((WIDE * SIDE, 4 * SIDE), bf16),
             pltpu.VMEM((4 * SIDE, WIDE * SIDE), bf16),
-            pltpu.SemaphoreType.DMA((own // WIDE // groups,)),
-            pltpu.SemaphoreType.DMA((6,)),
+            pltpu.VMEM((WIDE // 2, 2 * SIDE, 2 * SIDE), f32),
+            pltpu.VMEM((WIDE * SIDE, 2 * SIDE), f32),
+            pltpu.VMEM((4 * SIDE, 2 * SIDE), bf16),
+            pltpu.VMEM((6 * SIDE, 2 * SIDE), bf16),
+            pltpu.VMEM((6 * SIDE, 2 * SIDE), bf16),
+            pltpu.VMEM((2 * SIDE, 2 * SIDE), bf16),
+            pltpu.VMEM((2, SIDE, LANES), f32),
             pltpu.SemaphoreType.DMA((own // WIDE // groups,)),
         ],
-        compiler_params=streaming,
+        compiler_params=resident,
         name="mix",
-    )(message, weights, *known)
+    )(message, weights, known)
     message = lax.all_to_all(message, "seq", 0, 0)
 
     return pl.pallas_call(

time: 72.4 us -> 66.5 us (0.919)
  Pallas kernels: 24.6 us -> 18 us
  local copies, waits for them, and re-layouts: 3.35 us -> 5.02 us
    pallas_call x1, Pallas kernels: 12.5 us -> 9.54 us  [shards(): pl.pallas_call(mix_kernel, in_specs=[whole] * 3, out_specs=hbm, out_shape...]
    unnamed x18 -> x20, local copies, waits for them, and re-layouts: 2.68 us -> 4.93 us
    pallas_call x1, Pallas kernels: 6.44 us -> 4.38 us  [shards(): pl.pallas_call(gate_kernel, in_specs=[hbm] * 5, out_specs=hbm, out_shape=...]
    pallas_call x1, Pallas kernels: 3.37 us -> 1.8 us  [shards(): pl.pallas_call(join_kernel, in_specs=[whole] * 6, out_specs=hbm, out_shap...]
  transfers between devices with their start and end apart: 1 -> 1, of which waited for: 1 -> 1; matrix products, arithmetic and copies ran while one was open for 1% -> 0% of each run, Pallas kernels for 3% -> 3%
where the time goes in v1:
time: 66.5 us; the launch traced here: 66.2 us
  blocking collectives  22.3 us (34%)
  Pallas kernels  18 us (27%)
  waiting for transfers between devices  12.1 us (18%)
  starting transfers between devices  8.73 us (13%)
  local copies, waits for them, and re-layouts  5.02 us (8%)
    all_to_all x1, blocking collectives, shards(): message = lax.all_to_all(message, 'seq', 0, 0)  22.3 us
    all_to_all x1, waiting for transfers between devices, shards(): message = lax.all_to_all(message, 'seq', 0, 0)  12.1 us
    pallas_call x1, Pallas kernels, shards(): pl.pallas_call(mix_kernel, in_specs=[whole] * 3, out_specs=hbm, out_shape...  9.54 us
    all_to_all x1, starting transfers between devices, shards(): message = lax.all_to_all(message, 'seq', 0, 0)  8.73 us
    unnamed x20, local copies, waits for them, and re-layouts  4.93 us
    pallas_call x1, Pallas kernels, shards(): pl.pallas_call(gate_kernel, in_specs=[hbm] * 5, out_specs=hbm, out_shape=...  4.38 us
    pallas_call x1, Pallas kernels, shards(): pl.pallas_call(local_kernel, in_specs=[whole] * 5, out_specs=[whole] * 3,...  2.27 us
    pallas_call x1, Pallas kernels, shards(): pl.pallas_call(join_kernel, in_specs=[whole] * 6, out_specs=hbm, out_shap...  1.8 us
  transfers between devices with their start and end apart: 1, of which 1 were waited for; matrix products, arithmetic and copies ran while one was open for 0% of the time, Pallas kernels for 3%

profile of v1, /device:TPU:1, one launch (start us, length us, event | category | flops | bytes accessed | tf_op | source)
XLA Modules:
  0.0 66.2 jit_solution(10437079484063979733)
XLA Ops:
  0.0 4.4 %gate.1 = bf16[32,144,128]{2,1,0:T(8,128)(2,1)} custom-call(bf16[512,1024]{1,0:T(8,128)(2,1)} %q_ref, bf16[512,1024]{1,0:T(8,128)(2,1)} %k_ref, bf16[512,1024]{1,0:T(8,128)(2,1)} %v_ref, f32[3,3,1024]{2,1,0:T(4,128)} %w_ref.1, f32[64,512]{1,0:T(8,128)} %taps_hbm.1), custom_call_target="tpu_custom_call" | custom-call | tf_op jit(solution)/shard_map/gate/pallas_call | solution.py:553
  4.4 0.0 copy-start.8
  4.4 0.0 copy-start
  4.4 0.0 copy-start.1
  4.4 0.0 copy-start.9
  4.4 8.7 %all-to-all-start = ((bf16[32,144,128]{2,1,0:T(8,128)(2,1)}), bf16[32,144,128]{2,1,0:T(8,128)(2,1)S(1)}, u32[]{:S(2)}, u32[]{:S(2)}) async-start(bf16[32,144,128]{2,1,0:T(8,128)(2,1)} %gate.1), calls=%async_computation | async-start | bytes 2359296 | tf_op jit(solution)/shard_map/all_to_all | solution.py:578
  13.2 0.0 copy-done.8
  13.2 0.1 constant_dynamic-slice_fusion
  13.3 0.0 copy-done
  13.3 0.0 copy-done.1
  13.3 0.0 copy-done.9
  13.3 0.0 copy-start.2
  13.3 1.2 %copy-done.2 = bf16[512,1024]{1,0:T(8,128)(2,1)S(1)} copy-done((bf16[512,1024]{1,0:T(8,128)(2,1)S(1)}, bf16[512,1024]{1,0:T(8,128)(2,1)}, u32[]{:S(2)}) %copy-start.2) | copy-done | bytes 1048600
  14.5 2.3 %local.1 = (f32[512,1024]{1,0:T(8,128)S(1)}, f32[512,1024]{1,0:T(8,128)S(1)}, f32[8,1024]{1,0:T(8,128)S(1)}) custom-call(bf16[512,1024]{1,0:T(8,128)(2,1)S(1)} %copy-done, bf16[512,1024]{1,0:T(8,128)(2,1)S(1)} %copy-done.1, bf16[512,1024]{1,0:T(8,128)(2,1)S(1)} %copy-done.2, f32[3,3,1024]{2,1,0:T(4,128)S(1)} %copy-done.8, f32[1,1024]{1,0:T(1,128)S(1)} %bitcast.1), custom_call_target="tpu_custom_call" | custom-call | flops 10485760 | bytes 7340032 | tf_op jit(solution)/shard_map/local/pallas_call | solution.py:580
  16.8 0.0 copy-start.3
  16.8 1.3 %copy-done.3 = f32[512,1024]{1,0:T(8,128)} copy-done((f32[512,1024]{1,0:T(8,128)}, f32[512,1024]{1,0:T(8,128)S(1)}, u32[]{:S(2)}) %copy-start.3) | copy-done | bytes 2097176
  18.1 0.0 copy-start.5
  18.1 1.3 %copy-done.5 = f32[512,1024]{1,0:T(8,128)} copy-done((f32[512,1024]{1,0:T(8,128)}, f32[512,1024]{1,0:T(8,128)S(1)}, u32[]{:S(2)}) %copy-start.5) | copy-done | bytes 2097176
  19.4 12.1 %all-to-all-done.in_ref = bf16[32,144,128]{2,1,0:T(8,128)(2,1)S(1)} async-done(((bf16[32,144,128]{2,1,0:T(8,128)(2,1)}), bf16[32,144,128]{2,1,0:T(8,128)(2,1)S(1)}, u32[]{:S(2)}, u32[]{:S(2)}) %all-to-all-start) | async-done | bytes 1179680 | tf_op jit(solution)/shard_map/all_to_all | solution.py:578
  31.5 0.0 copy-start.7
  31.5 1.0 %copy-done.7 = bf16[2048,128]{1,0:T(8,128)(2,1)S(1)} copy-done((bf16[2048,128]{1,0:T(8,128)(2,1)S(1)}, bf16[2048,128]{1,0:T(8,128)(2,1)}, u32[]{:S(2)}) %copy-start.7) | copy-done | bytes 524312
  32.6 0.0 copy-start.6
  32.6 9.5 %mix.1 = bf16[32,136,128]{2,1,0:T(8,128)(2,1)S(1)} custom-call(bf16[32,144,128]{2,1,0:T(8,128)(2,1)S(1)} %all-to-all-done.in_ref, f32[3,3,128]{2,1,0:T(4,128)S(1)} %pad.4.w_ref, bf16[2048,128]{1,0:T(8,128)(2,1)S(1)} %copy-done.7), custom_call_target="tpu_custom_call" | custom-call | tf_op jit(solution)/shard_map/mix/pallas_call | solution.py:602
  42.1 0.0 copy-start.4
  42.1 22.3 %all_to_all.10.in_ref = bf16[32,136,128]{2,1,0:T(8,128)(2,1)S(1)} all-to-all(bf16[32,136,128]{2,1,0:T(8,128)(2,1)S(1)} %mix.1), channel_id=1, replica_groups=mesh['seq'=32,'ch'=8] {'seq'}, dimensions={0} | all-to-all | bytes 2228224 | tf_op jit(solution)/shard_map/all_to_all | solution.py:632
  64.4 0.0 copy-done.6
  64.4 0.0 copy-done.4
  64.4 1.8 %join.1 = bf16[512,1024]{1,0:T(8,128)(2,1)} custom-call(bf16[32,136,128]{2,1,0:T(8,128)(2,1)S(1)} %all_to_all.10.in_ref, f32[512,1024]{1,0:T(8,128)S(1)} %copy-done.4, f32[512,1024]{1,0:T(8,128)S(1)} %copy-done.6, f32[8,1024]{1,0:T(8,128)S(1)} %get-tuple-element.34.ends_ref, f32[3,3,1024]{2,1,0:T(4,128)S(1)} %copy-done.8, f32[1,1024]{1,0:T(1,128)S(1)} %bitcast.2), custom_call_target="tpu_custom_call" | custom-call | tf_op jit(solution)/shard_map/join/pallas_call | solution.py:634
  (1 shorter events, 0.0 us)
Async XLA Ops:
  4.4 8.8 %copy-start.8 = (f32[3,3,1024]{2,1,0:T(4,128)S(1)}, f32[3,3,1024]{2,1,0:T(4,128)}, u32[]{:S(2)}) copy-start(f32[3,3,1024]{2,1,0:T(4,128)} %w_ref.1) | copy-start | bytes 110596
  4.4 8.9 %copy-start = (bf16[512,1024]{1,0:T(8,128)(2,1)S(1)}, bf16[512,1024]{1,0:T(8,128)(2,1)}, u32[]{:S(2)}) copy-start(bf16[512,1024]{1,0:T(8,128)(2,1)} %q_ref) | copy-start | bytes 3145732
  4.4 8.9 %copy-start.1 = (bf16[512,1024]{1,0:T(8,128)(2,1)S(1)}, bf16[512,1024]{1,0:T(8,128)(2,1)}, u32[]{:S(2)}) copy-start(bf16[512,1024]{1,0:T(8,128)(2,1)} %k_ref) | copy-start | bytes 3145732
  4.4 8.9 %copy-start.9 = (f32[1024]{0:T(1024)S(1)}, f32[1024]{0:T(1024)}, u32[]{:S(2)}) copy-start(f32[1024]{0:T(1024)} %param.11) | copy-start | bytes 12292
  4.4 27.1 %all-to-all-start = ((bf16[32,144,128]{2,1,0:T(8,128)(2,1)}), bf16[32,144,128]{2,1,0:T(8,128)(2,1)S(1)}, u32[]{:S(2)}, u32[]{:S(2)}) async-start(bf16[32,144,128]{2,1,0:T(8,128)(2,1)} %gate.1), calls=%async_computation | async-start | bytes 2359296 | tf_op jit(solution)/shard_map/all_to_all | solution.py:578
  13.3 1.2 %copy-start.2 = (bf16[512,1024]{1,0:T(8,128)(2,1)S(1)}, bf16[512,1024]{1,0:T(8,128)(2,1)}, u32[]{:S(2)}) copy-start(bf16[512,1024]{1,0:T(8,128)(2,1)} %v_ref) | copy-start | bytes 3145732
  16.8 1.3 %copy-start.3 = (f32[512,1024]{1,0:T(8,128)}, f32[512,1024]{1,0:T(8,128)S(1)}, u32[]{:S(2)}) copy-start(f32[512,1024]{1,0:T(8,128)S(1)} %get-tuple-element.32.q_ref) | copy-start | bytes 6291460
  18.1 1.3 %copy-start.5 = (f32[512,1024]{1,0:T(8,128)}, f32[512,1024]{1,0:T(8,128)S(1)}, u32[]{:S(2)}) copy-start(f32[512,1024]{1,0:T(8,128)S(1)} %get-tuple-element.33.s_ref) | copy-start | bytes 6291460
  31.5 1.0 %copy-start.7 = (bf16[2048,128]{1,0:T(8,128)(2,1)S(1)}, bf16[2048,128]{1,0:T(8,128)(2,1)}, u32[]{:S(2)}) copy-start(bf16[2048,128]{1,0:T(8,128)(2,1)} %constant.16.clone.table_ref) | copy-start | bytes 1572868
  32.6 31.8 %copy-start.6 = (f32[512,1024]{1,0:T(8,128)S(1)}, f32[512,1024]{1,0:T(8,128)}, u32[]{:S(2)}) copy-start(f32[512,1024]{1,0:T(8,128)} %copy-done.5) | copy-start | bytes 6291460
  42.1 22.3 %copy-start.4 = (f32[512,1024]{1,0:T(8,128)S(1)}, f32[512,1024]{1,0:T(8,128)}, u32[]{:S(2)}) copy-start(f32[512,1024]{1,0:T(8,128)} %copy-done.3) | copy-start | bytes 6291460

commit v2 on v1

--- a/solution.py
+++ b/solution.py
@@ -11,13 +11,14 @@
 GROUP_SIZE = 16
 SIDE = 128
 LANES = 128
-LAGS = 6
+LAGS = 7
 WIDE = 4
 CODE_POWER = 17
 CODE_TOP = 2.0 ** (120.0 / CODE_POWER)
 CODE_LEAST = 2.0**-126
 INV_LN2 = 1.0 / math.log(2.0)
 RESIDENT_LIMIT = 12 * 1024 * 1024
+MIX_LIMIT = 20 * 1024 * 1024
 STREAMING_LIMIT = 60 * 1024 * 1024
 
 f32, bf16 = jnp.float32, jnp.bfloat16
@@ -93,6 +94,7 @@
     q_ends,
     taps_in,
     sems,
+    last_sems,
 ):
     rows, channels = k_buf.shape
     steps = rows // SIDE
@@ -109,9 +111,14 @@
         return pltpu.make_async_copy(source.at[span], target.at[span], sems.at[at, step])
 
     def out_copy(step):
-        end = base + 16 if step == steps - 1 else (step + 1) * per
-        span = pl.ds(step * per, end - step * per)
+        span = pl.ds(step * per, per)
         return pltpu.make_async_copy(out_ref.at[:, span], out_hbm.at[:, span], sems.at[3, step])
+
+    def last_copy(block):
+        dest, span = pl.ds(block * dests, dests), pl.ds(base - per, per + 16)
+        return pltpu.make_async_copy(
+            out_ref.at[dest, span], out_hbm.at[dest, span], last_sems.at[block]
+        )
 
     w_copy = pltpu.make_async_copy(w_hbm, w_buf, sems.at[2, 0])
     taps_copy = pltpu.make_async_copy(taps_hbm, taps_buf, sems.at[2, 1])
@@ -152,9 +159,9 @@
             span = slice(block * dests, (block + 1) * dests)
             out_ref[span, step * per : (step + 1) * per, :] = code.reshape(dests, per, LANES)
 
-        for block in range(blocks):
-            tile(block)
         if step < steps - 1:
+            for block in range(blocks):
+                tile(block)
             out_copy(step).start()
 
     def tail(block):
@@ -191,10 +198,15 @@
     scales[steps:, :] = jnp.zeros((8 - steps, channels), f32)
     q_ends[...] = jnp.zeros_like(q_ends)
     for block in range(blocks):
+        tile(block)
         tail(block)
-    out_copy(steps - 1).start()
-    for step in range(steps):
+        if block % 2 == 1:
+            last_copy(block - 1).start()
+            last_copy(block).start()
+    for step in range(steps - 1):
         out_copy(step).wait()
+    for block in range(blocks):
+        last_copy(block).wait()
 
 
 def mix_kernel(
@@ -219,6 +231,7 @@
     unturned,
     first_raw,
     third_raw,
+    fourth_raw,
     first,
     second,
     third,
@@ -303,10 +316,17 @@
             asked = pltpu.roll(tails[pl.ds(at, blocks, stride=8), :], LANES - 3 * channels, 1)
             asked = jnp.where(block == 0, 0.0, pltpu.roll(asked, 1, 0))
             back_tails[pl.ds(1 + at, blocks, stride=8), :] = asked
-        packed = [shorts[0][token] * shorts[1][token] for token in range(2)]
+        from_lane = lax.broadcasted_iota(jnp.int32, (LANES, LANES), 0)
+        to_lane = lax.broadcasted_iota(jnp.int32, (LANES, LANES), 1)
+        known = lax.broadcasted_iota(jnp.int32, (blocks, LANES), 1) < channels
+        spread = jnp.zeros((blocks, LANES), f32)
         for token in range(2):
-            starts[token] = jnp.zeros((SIDE, LANES), f32)
-            starts[token, pl.ds(0, blocks, stride=per_block), :] = packed[token]
+            gated = jnp.where(known, shorts[0][token] * shorts[1][token], 0.0)
+            place = jnp.where(to_lane == 2 * from_lane + token, 1.0, 0.0).astype(bf16)
+            for part in halves(gated):
+                spread = spread + dot(part, place)
+        starts[...] = jnp.zeros((SIDE, LANES), f32)
+        starts[pl.ds(0, blocks, stride=per_block), :] = spread
 
     gated_starts()
 
@@ -322,20 +342,17 @@
         return dot(ref[:rows], table[: 4 * SIDE]) + dot(ref[:rows, : 2 * SIDE], table[4 * SIDE :])
 
     lane = lax.broadcasted_iota(jnp.int32, (SIDE, LANES), 1)
-    starts_block = lax.broadcasted_iota(jnp.int32, (SIDE, LANES), 0) % per_block == 0
-    start_masks = [starts_block & (lane == token) for token in range(2)]
+    is_start = (lax.broadcasted_iota(jnp.int32, (SIDE, LANES), 0) % per_block == 0) & (lane < 2)
 
     def load(n, group):
         level = pltpu.roll(levels[...], LANES - channels - WIDE * n, 1) * (1.0 / CODE_TOP)
-        first_tokens = [pltpu.roll(starts[token], LANES - WIDE * n, 1) for token in range(2)]
         at = WIDE * (n - group * slots)
         values = []
         for i in range(WIDE):
             code = signals[group][pl.ds(at + i, SIDE, stride=GROUP_SIZE), :]
             value = decode(code, level[:, i : i + 1])
-            for token in range(2):
-                value = jnp.where(start_masks[token], first_tokens[token][:, i : i + 1], value)
-            values.append(value)
+            start = pltpu.roll(starts[...], (LANES - 2 * (WIDE * n + i)) % LANES, 1)
+            values.append(jnp.where(is_start, start, value))
         return values
 
     def first_side(values):
@@ -373,18 +390,16 @@
             unturned[2 * SIDE :, at * SIDE : (at + 1) * SIDE] = low
 
     def first_side_back():
-        found = []
         for pair in range(WIDE // 2):
             span = slice(2 * pair * SIDE, (2 * pair + 2) * SIDE)
             done = dot(fourth[...], unturned[: 2 * SIDE, span])
-            found.append(
+            fourth_raw[pair] = (
                 done[:SIDE] + done[SIDE:] + dot(fourth[:SIDE], unturned[2 * SIDE :, span])
             )
-        return found
-
-    def finish(n, group, found):
+
+    def finish(n, group):
         for i in range(WIDE):
-            value = found[i // 2][:, i % 2 * SIDE : (i % 2 + 1) * SIDE]
+            value = fourth_raw[i // 2, :, i % 2 * SIDE : (i % 2 + 1) * SIDE]
             top = jnp.max(jnp.max(jnp.abs(value), axis=0, keepdims=True), axis=1, keepdims=True)
             scale = code_scale(top)
             channel = WIDE * n + i
@@ -393,11 +408,13 @@
             results[group][place, :] = encode(value, CODE_TOP / scale)
 
     def step(n, load_group, finish_group, active=(True,) * LAGS):
-        loads, turns, filters, filtered_back, turns_back, finishes = active
+        loads, turns, filters, filtered_back, turns_back, sides_back, finishes = active
+        if finishes:
+            finish(n - 6, finish_group)
         if filters:
             spectrum = table_right(turned, second)
-        if finishes:
-            found = first_side_back()
+        if sides_back:
+            first_side_back()
         if turns:
             turn()
         if turns_back:
@@ -406,39 +423,38 @@
             third_raw[...] = table_right(filtered, third)
         if loads:
             first_side(load(n, load_group))
-        if finishes:
-            finish(n - 5, finish_group, found)
         if filters:
             filter_spectrum(n - 2, spectrum)
 
-    def pack(slot, group):
+    def pack(slot, half):
+        group, above = half // 2, half % 2 * 8
         for i in range(slot_blocks):
             j = slot * slot_blocks + i
             for a in range(per_block):
-                at = a * channels + group * GROUP_SIZE
-                place = (j * per_block + a) * GROUP_SIZE
-                code = results[group][place : place + GROUP_SIZE, :]
-                out_ref[j, at : at + GROUP_SIZE, :] = code.astype(bf16)
+                at = a * channels + group * GROUP_SIZE + above
+                place = (j * per_block + a) * GROUP_SIZE + above
+                code = results[group][place : place + 8, :]
+                out_ref[j, at : at + 8, :] = code.astype(bf16)
 
     first_side([taps[pl.ds(g, SIDE, stride=groups), :] for g in range(groups)])
     turn(groups)
     spectra[...] = table_right(turned, second, groups).reshape(groups, SIDE, 2 * SIDE) * (
         1.0 / (SIDE * SIDE)
     )
-    for n in range(slots):
-        step(n, 0, 0, tuple(n >= lag for lag in range(LAGS)))
-        unpack(n, 1)
-    step(slots, 1, 0, tuple(slots >= lag for lag in range(LAGS)))
+    for n in range(LAGS - 1):
+        step(n, n // slots, 0, tuple(n >= lag for lag in range(LAGS)))
+        if n < slots:
+            unpack(n, 1)
 
     def steady(n, carry):
         step(n, 1, 0)
         return carry
 
-    lax.fori_loop(slots + 1, count, steady, 0)
+    lax.fori_loop(LAGS - 1, count, steady, 0)
     for n in range(count, count + LAGS - 1):
-        step(n, 1, int(n - LAGS + 1 >= slots), tuple(n - lag < count for lag in range(LAGS)))
-        if n > count:
-            pack(n - count - 1, 0)
+        step(n, 1, (n - 6) // slots, tuple(n - lag < count for lag in range(LAGS)))
+        for slot in range(slots // 2):
+            pack((n - count) % 2 * (slots // 2) + slot, (n - count) // 2)
 
     diagonal = lax.broadcasted_iota(jnp.int32, (channels, LANES), 1) == lax.broadcasted_iota(
         jnp.int32, (channels, LANES), 0
@@ -448,7 +464,7 @@
     back_tails[pl.ds(7, blocks, stride=8), :] = jnp.zeros((blocks, LANES), f32)
     out_ref[:, data : data + 8, :] = back_tails[...].reshape(blocks, 8, LANES).astype(bf16)
     for slot in range(slots):
-        pack(slot, 1)
+        pack(slot, 2 * groups - 1)
         out_copy(slot).start()
     for slot in range(slots):
         out_copy(slot).wait()
@@ -568,6 +584,7 @@
             pltpu.VMEM((blocks, 8, LANES), f32),
             pltpu.VMEM((blocks, 2 * steps * filter_taps.shape[0] // blocks, LANES), f32),
             pltpu.SemaphoreType.DMA((4, steps)),
+            pltpu.SemaphoreType.DMA((blocks,)),
         ],
         compiler_params=streaming,
         name="gate",
@@ -587,7 +604,7 @@
             jax.ShapeDtypeStruct((8, channels), f32),
         ],
         scratch_shapes=[pltpu.VMEM((3, 16 + SIDE, LANES), f32)],
-        compiler_params=resident,
+        compiler_params=streaming,
         cost_estimate=pl.CostEstimate(
             flops=20 * rows * channels, bytes_accessed=14 * rows * channels, transcendentals=0
         ),
@@ -613,12 +630,13 @@
             pltpu.VMEM((seq * 8, LANES), f32),
             pltpu.VMEM((seq * 8, LANES), f32),
             pltpu.VMEM((SIDE, LANES), f32),
-            pltpu.VMEM((2, SIDE, LANES), f32),
+            pltpu.VMEM((SIDE, LANES), f32),
             pltpu.VMEM((WIDE * SIDE, 4 * SIDE), bf16),
             pltpu.VMEM((WIDE * SIDE, 4 * SIDE), bf16),
             pltpu.VMEM((4 * SIDE, WIDE * SIDE), bf16),
             pltpu.VMEM((WIDE // 2, 2 * SIDE, 2 * SIDE), f32),
             pltpu.VMEM((WIDE * SIDE, 2 * SIDE), f32),
+            pltpu.VMEM((WIDE // 2, SIDE, 2 * SIDE), f32),
             pltpu.VMEM((4 * SIDE, 2 * SIDE), bf16),
             pltpu.VMEM((6 * SIDE, 2 * SIDE), bf16),
             pltpu.VMEM((6 * SIDE, 2 * SIDE), bf16),
@@ -626,7 +644,7 @@
             pltpu.VMEM((2, SIDE, LANES), f32),
             pltpu.SemaphoreType.DMA((own // WIDE // groups,)),
         ],
-        compiler_params=resident,
+        compiler_params=pltpu.CompilerParams(vmem_limit_bytes=MIX_LIMIT),
         name="mix",
     )(message, weights, known)
     message = lax.all_to_all(message, "seq", 0, 0)

time: 66.5 us -> 65.1 us (0.979)
  local copies, waits for them, and re-layouts: 5.02 us -> 0.81 us
  Pallas kernels: 18 us -> 21.7 us
  waiting for transfers between devices: 12.1 us -> 11.4 us
    unnamed x20 -> x12, local copies, waits for them, and re-layouts: 4.93 us -> 0.03 us
    pallas_call x1, Pallas kernels: 2.27 us -> 6.17 us  [shards(): pl.pallas_call(local_kernel, in_specs=[whole] * 5, out_specs=[whole] * 3,...]
    dynamic_slice x1, local copies, waits for them, and re-layouts: 0.08 us -> 0.77 us  [shards(): lax.dynamic_slice_in_dim(short_weight, lax.axis_index('seq') * own, own,...]
    all_to_all x1, waiting for transfers between devices: 12.1 us -> 11.4 us  [shards(): message = lax.all_to_all(message, 'seq', 0, 0)]
  transfers between devices with their start and end apart: 1 -> 1, of which waited for: 1 -> 1; matrix products, arithmetic and copies ran while one was open for 0% -> 1% of each run, Pallas kernels for 3% -> 10%
where the time goes in v2:
time: 65.1 us; the launch traced here: 64.8 us
  blocking collectives  22.3 us (34%)
  Pallas kernels  21.7 us (33%)
  waiting for transfers between devices  11.4 us (18%)
  starting transfers between devices  8.6 us (13%)
  local copies, waits for them, and re-layouts  0.81 us (1%)
    all_to_all x1, blocking collectives, shards(): message = lax.all_to_all(message, 'seq', 0, 0)  22.3 us
    all_to_all x1, waiting for transfers between devices, shards(): message = lax.all_to_all(message, 'seq', 0, 0)  11.4 us
    pallas_call x1, Pallas kernels, shards(): pl.pallas_call(mix_kernel, in_specs=[whole] * 3, out_specs=hbm, out_shape...  9.36 us
    all_to_all x1, starting transfers between devices, shards(): message = lax.all_to_all(message, 'seq', 0, 0)  8.6 us
    pallas_call x1, Pallas kernels, shards(): pl.pallas_call(local_kernel, in_specs=[whole] * 5, out_specs=[whole] * 3,...  6.17 us
    pallas_call x1, Pallas kernels, shards(): pl.pallas_call(gate_kernel, in_specs=[hbm] * 5, out_specs=hbm, out_shape=...  4.34 us
    pallas_call x1, Pallas kernels, shards(): pl.pallas_call(join_kernel, in_specs=[whole] * 6, out_specs=hbm, out_shap...  1.79 us
  transfers between devices with their start and end apart: 1, of which 1 were waited for; matrix products, arithmetic and copies ran while one was open for 1% of the time, Pallas kernels for 10%

profile of v2, /device:TPU:1, one launch (start us, length us, event | category | flops | bytes accessed | tf_op | source)
XLA Modules:
  0.0 64.8 jit_solution(14822297995875493208)
XLA Ops:
  0.0 4.3 %gate.1 = bf16[32,144,128]{2,1,0:T(8,128)(2,1)} custom-call(bf16[512,1024]{1,0:T(8,128)(2,1)} %q_ref, bf16[512,1024]{1,0:T(8,128)(2,1)} %k_ref, bf16[512,1024]{1,0:T(8,128)(2,1)} %v_ref, f32[3,3,1024]{2,1,0:T(4,128)} %w_ref.1, f32[64,512]{1,0:T(8,128)} %taps_hbm.1), custom_call_target="tpu_custom_call" | custom-call | tf_op jit(solution)/shard_map/gate/pallas_call | solution.py:569
  4.3 8.6 %all-to-all-start = ((bf16[32,144,128]{2,1,0:T(8,128)(2,1)}), bf16[32,144,128]{2,1,0:T(8,128)(2,1)S(1)}, u32[]{:S(2)}, u32[]{:S(2)}) async-start(bf16[32,144,128]{2,1,0:T(8,128)(2,1)} %gate.1), calls=%async_computation | async-start | bytes 2359296 | tf_op jit(solution)/shard_map/all_to_all | solution.py:595
  13.0 0.8 %constant_dynamic-slice_fusion = f32[3,3,32]{2,1,0:T(4,128)S(1)} fusion(f32[3,3,1024]{2,1,0:T(4,128)} %w_ref.1, s32[]{:T(128)S(6)} %select_n.3), kind=kLoop, calls=%fused_computation | loop fusion | bytes 2308 | tf_op jit(solution)/shard_map/dynamic_slice | solution.py:613
  13.7 0.0 copy-start.2
  13.7 6.2 %local.1 = (f32[512,1024]{1,0:T(8,128)}, f32[512,1024]{1,0:T(8,128)}, f32[8,1024]{1,0:T(8,128)}) custom-call(bf16[512,1024]{1,0:T(8,128)(2,1)} %q_ref, bf16[512,1024]{1,0:T(8,128)(2,1)} %k_ref, bf16[512,1024]{1,0:T(8,128)(2,1)} %v_ref, f32[3,3,1024]{2,1,0:T(4,128)} %w_ref.1, f32[1,1024]{1,0:T(1,128)} %bitcast.1), custom_call_target="tpu_custom_call" | custom-call | flops 10485760 | bytes 7340032 | tf_op jit(solution)/shard_map/local/pallas_call | solution.py:597
  19.9 11.4 %all-to-all-done.in_ref = bf16[32,144,128]{2,1,0:T(8,128)(2,1)S(1)} async-done(((bf16[32,144,128]{2,1,0:T(8,128)(2,1)}), bf16[32,144,128]{2,1,0:T(8,128)(2,1)S(1)}, u32[]{:S(2)}, u32[]{:S(2)}) %all-to-all-start) | async-done | bytes 1179680 | tf_op jit(solution)/shard_map/all_to_all | solution.py:595
  31.3 0.0 copy-done.2
  31.3 0.0 copy-start.1
  31.3 9.4 %mix.1 = bf16[32,136,128]{2,1,0:T(8,128)(2,1)S(1)} custom-call(bf16[32,144,128]{2,1,0:T(8,128)(2,1)S(1)} %all-to-all-done.in_ref, f32[3,3,128]{2,1,0:T(4,128)S(1)} %pad.4.w_ref, bf16[2048,128]{1,0:T(8,128)(2,1)S(1)} %copy-done.2), custom_call_target="tpu_custom_call" | custom-call | tf_op jit(solution)/shard_map/mix/pallas_call | solution.py:619
  40.7 0.0 copy-start
  40.7 0.0 copy-start.3
  40.7 0.0 copy-start.4
  40.7 0.0 copy-start.5
  40.7 22.3 %all_to_all.10.in_ref = bf16[32,136,128]{2,1,0:T(8,128)(2,1)S(1)} all-to-all(bf16[32,136,128]{2,1,0:T(8,128)(2,1)S(1)} %mix.1), channel_id=1, replica_groups=mesh['seq'=32,'ch'=8] {'seq'}, dimensions={0} | all-to-all | bytes 2228224 | tf_op jit(solution)/shard_map/all_to_all | solution.py:650
  63.0 0.0 copy-done.1
  63.0 0.0 copy-done
  63.0 0.0 copy-done.3
  63.0 0.0 copy-done.4
  63.0 0.0 copy-done.5
  63.0 1.8 %join.1 = bf16[512,1024]{1,0:T(8,128)(2,1)} custom-call(bf16[32,136,128]{2,1,0:T(8,128)(2,1)S(1)} %all_to_all.10.in_ref, f32[512,1024]{1,0:T(8,128)S(1)} %copy-done, f32[512,1024]{1,0:T(8,128)S(1)} %copy-done.1, f32[8,1024]{1,0:T(8,128)S(1)} %copy-done.4, f32[3,3,1024]{2,1,0:T(4,128)S(1)} %copy-done.3, f32[1,1024]{1,0:T(1,128)S(1)} %bitcast.2), custom_call_target="tpu_custom_call" | custom-call | tf_op jit(solution)/shard_map/join/pallas_call | solution.py:652
  (1 shorter events, 0.0 us)
Async XLA Ops:
  4.3 27.0 %all-to-all-start = ((bf16[32,144,128]{2,1,0:T(8,128)(2,1)}), bf16[32,144,128]{2,1,0:T(8,128)(2,1)S(1)}, u32[]{:S(2)}, u32[]{:S(2)}) async-start(bf16[32,144,128]{2,1,0:T(8,128)(2,1)} %gate.1), calls=%async_computation | async-start | bytes 2359296 | tf_op jit(solution)/shard_map/all_to_all | solution.py:595
  13.7 17.6 %copy-start.2 = (bf16[2048,128]{1,0:T(8,128)(2,1)S(1)}, bf16[2048,128]{1,0:T(8,128)(2,1)}, u32[]{:S(2)}) copy-start(bf16[2048,128]{1,0:T(8,128)(2,1)} %constant.16.clone.table_ref) | copy-start | bytes 1572868
  31.3 31.7 %copy-start.1 = (f32[512,1024]{1,0:T(8,128)S(1)}, f32[512,1024]{1,0:T(8,128)}, u32[]{:S(2)}) copy-start(f32[512,1024]{1,0:T(8,128)} %get-tuple-element.33.s_ref) | copy-start | bytes 6291460
  40.7 22.3 %copy-start = (f32[512,1024]{1,0:T(8,128)S(1)}, f32[512,1024]{1,0:T(8,128)}, u32[]{:S(2)}) copy-start(f32[512,1024]{1,0:T(8,128)} %get-tuple-element.32.q_ref) | copy-start | bytes 6291460
  40.7 22.3 %copy-start.3 = (f32[3,3,1024]{2,1,0:T(4,128)S(1)}, f32[3,3,1024]{2,1,0:T(4,128)}, u32[]{:S(2)}) copy-start(f32[3,3,1024]{2,1,0:T(4,128)} %w_ref.1) | copy-start | bytes 110596
  40.7 22.3 %copy-start.4 = (f32[8,1024]{1,0:T(8,128)S(1)}, f32[8,1024]{1,0:T(8,128)}, u32[]{:S(2)}) copy-start(f32[8,1024]{1,0:T(8,128)} %get-tuple-element.34.ends_ref) | copy-start | bytes 98308
  40.7 22.3 %copy-start.5 = (f32[1024]{0:T(1024)S(1)}, f32[1024]{0:T(1024)}, u32[]{:S(2)}) copy-start(f32[1024]{0:T(1024)} %param.11) | copy-start | bytes 12292

commit v3 on v2

--- a/solution.py
+++ b/solution.py
@@ -358,8 +358,8 @@
     def first_side(values):
         for pair in range(len(values) // 2):
             high, low = halves(jnp.concatenate(values[2 * pair : 2 * pair + 2], axis=1))
-            wide = dot(first[...], jnp.concatenate([high, low], axis=0))
-            first_raw[pair] = wide[: 2 * SIDE] + wide[2 * SIDE :]
+            both = jnp.concatenate([high, low], axis=0)
+            first_raw[pair] = dot(first[: 2 * SIDE], both) + dot(first[2 * SIDE :, :SIDE], high)
 
     def turn(used=WIDE):
         for at in range(used):
@@ -411,20 +411,20 @@
         loads, turns, filters, filtered_back, turns_back, sides_back, finishes = active
         if finishes:
             finish(n - 6, finish_group)
+        if sides_back:
+            first_side_back()
+        if turns_back:
+            turn_back()
         if filters:
             spectrum = table_right(turned, second)
-        if sides_back:
-            first_side_back()
         if turns:
             turn()
-        if turns_back:
-            turn_back()
         if filtered_back:
             third_raw[...] = table_right(filtered, third)
+        if filters:
+            filter_spectrum(n - 2, spectrum)
         if loads:
             first_side(load(n, load_group))
-        if filters:
-            filter_spectrum(n - 2, spectrum)
 
     def pack(slot, half):
         group, above = half // 2, half % 2 * 8
@@ -446,11 +446,8 @@
         if n < slots:
             unpack(n, 1)
 
-    def steady(n, carry):
+    for n in range(LAGS - 1, count):
         step(n, 1, 0)
-        return carry
-
-    lax.fori_loop(LAGS - 1, count, steady, 0)
     for n in range(count, count + LAGS - 1):
         step(n, 1, (n - 6) // slots, tuple(n - lag < count for lag in range(LAGS)))
         for slot in range(slots // 2):
@@ -582,7 +579,7 @@
             pltpu.VMEM((8, channels), f32),
             pltpu.VMEM((blocks, 8, LANES), f32),
             pltpu.VMEM((blocks, 8, LANES), f32),
-            pltpu.VMEM((blocks, 2 * steps * filter_taps.shape[0] // blocks, LANES), f32),
+            pltpu.VMEM((blocks + 1, 2 * steps * filter_taps.shape[0] // blocks, LANES), f32),
             pltpu.SemaphoreType.DMA((4, steps)),
             pltpu.SemaphoreType.DMA((blocks,)),
         ],

time: 65.1 us -> 64.5 us (level)
  no operation moved by 1% of the time
where the time goes in v3:
time: 64.5 us; the launch traced here: 64.2 us
  blocking collectives  22.3 us (35%)
  Pallas kernels  21.1 us (33%)
  waiting for transfers between devices  11.4 us (18%)
  starting transfers between devices  8.6 us (13%)
  local copies, waits for them, and re-layouts  0.81 us (1%)
    all_to_all x1, blocking collectives, shards(): message = lax.all_to_all(message, 'seq', 0, 0)  22.3 us
    all_to_all x1, waiting for transfers between devices, shards(): message = lax.all_to_all(message, 'seq', 0, 0)  11.4 us
    pallas_call x1, Pallas kernels, shards(): pl.pallas_call(mix_kernel, in_specs=[whole] * 3, out_specs=hbm, out_shape...  8.79 us
    all_to_all x1, starting transfers between devices, shards(): message = lax.all_to_all(message, 'seq', 0, 0)  8.6 us
    pallas_call x1, Pallas kernels, shards(): pl.pallas_call(local_kernel, in_specs=[whole] * 5, out_specs=[whole] * 3,...  6.17 us
    pallas_call x1, Pallas kernels, shards(): pl.pallas_call(gate_kernel, in_specs=[hbm] * 5, out_specs=hbm, out_shape=...  4.34 us
    pallas_call x1, Pallas kernels, shards(): pl.pallas_call(join_kernel, in_specs=[whole] * 6, out_specs=hbm, out_shap...  1.79 us
  transfers between devices with their start and end apart: 1, of which 1 were waited for; matrix products, arithmetic and copies ran while one was open for 1% of the time, Pallas kernels for 10%

profile of v3, /device:TPU:1, one launch (start us, length us, event | category | flops | bytes accessed | tf_op | source)
XLA Modules:
  0.0 64.2 jit_solution(6897786758739064501)
XLA Ops:
  0.0 4.3 %gate.1 = bf16[32,144,128]{2,1,0:T(8,128)(2,1)} custom-call(bf16[512,1024]{1,0:T(8,128)(2,1)} %q_ref, bf16[512,1024]{1,0:T(8,128)(2,1)} %k_ref, bf16[512,1024]{1,0:T(8,128)(2,1)} %v_ref, f32[3,3,1024]{2,1,0:T(4,128)} %w_ref.1, f32[64,512]{1,0:T(8,128)} %taps_hbm.1), custom_call_target="tpu_custom_call" | custom-call | tf_op jit(solution)/shard_map/gate/pallas_call | solution.py:566
  4.3 8.6 %all-to-all-start = ((bf16[32,144,128]{2,1,0:T(8,128)(2,1)}), bf16[32,144,128]{2,1,0:T(8,128)(2,1)S(1)}, u32[]{:S(2)}, u32[]{:S(2)}) async-start(bf16[32,144,128]{2,1,0:T(8,128)(2,1)} %gate.1), calls=%async_computation | async-start | bytes 2359296 | tf_op jit(solution)/shard_map/all_to_all | solution.py:592
  13.0 0.8 %constant_dynamic-slice_fusion = f32[3,3,32]{2,1,0:T(4,128)S(1)} fusion(f32[3,3,1024]{2,1,0:T(4,128)} %w_ref.1, s32[]{:T(128)S(6)} %select_n.3), kind=kLoop, calls=%fused_computation | loop fusion | bytes 2308 | tf_op jit(solution)/shard_map/dynamic_slice | solution.py:610
  13.7 0.0 copy-start.2
  13.7 6.2 %local.1 = (f32[512,1024]{1,0:T(8,128)}, f32[512,1024]{1,0:T(8,128)}, f32[8,1024]{1,0:T(8,128)}) custom-call(bf16[512,1024]{1,0:T(8,128)(2,1)} %q_ref, bf16[512,1024]{1,0:T(8,128)(2,1)} %k_ref, bf16[512,1024]{1,0:T(8,128)(2,1)} %v_ref, f32[3,3,1024]{2,1,0:T(4,128)} %w_ref.1, f32[1,1024]{1,0:T(1,128)} %bitcast.1), custom_call_target="tpu_custom_call" | custom-call | flops 10485760 | bytes 7340032 | tf_op jit(solution)/shard_map/local/pallas_call | solution.py:594
  19.9 11.4 %all-to-all-done.in_ref = bf16[32,144,128]{2,1,0:T(8,128)(2,1)S(1)} async-done(((bf16[32,144,128]{2,1,0:T(8,128)(2,1)}), bf16[32,144,128]{2,1,0:T(8,128)(2,1)S(1)}, u32[]{:S(2)}, u32[]{:S(2)}) %all-to-all-start) | async-done | bytes 1179680 | tf_op jit(solution)/shard_map/all_to_all | solution.py:592
  31.3 0.0 copy-done.2
  31.3 0.0 copy-start.1
  31.3 8.8 %mix.1 = bf16[32,136,128]{2,1,0:T(8,128)(2,1)S(1)} custom-call(bf16[32,144,128]{2,1,0:T(8,128)(2,1)S(1)} %all-to-all-done.in_ref, f32[3,3,128]{2,1,0:T(4,128)S(1)} %pad.4.w_ref, bf16[2048,128]{1,0:T(8,128)(2,1)S(1)} %copy-done.2), custom_call_target="tpu_custom_call" | custom-call | tf_op jit(solution)/shard_map/mix/pallas_call | solution.py:616
  40.1 0.0 copy-start
  40.1 0.0 copy-start.3
  40.1 0.0 copy-start.4
  40.1 0.0 copy-start.5
  40.2 22.3 %all_to_all.10.in_ref = bf16[32,136,128]{2,1,0:T(8,128)(2,1)S(1)} all-to-all(bf16[32,136,128]{2,1,0:T(8,128)(2,1)S(1)} %mix.1), channel_id=1, replica_groups=mesh['seq'=32,'ch'=8] {'seq'}, dimensions={0} | all-to-all | bytes 2228224 | tf_op jit(solution)/shard_map/all_to_all | solution.py:647
  62.4 0.0 copy-done.1
  62.4 0.0 copy-done
  62.4 0.0 copy-done.3
  62.4 0.0 copy-done.4
  62.4 0.0 copy-done.5
  62.4 1.8 %join.1 = bf16[512,1024]{1,0:T(8,128)(2,1)} custom-call(bf16[32,136,128]{2,1,0:T(8,128)(2,1)S(1)} %all_to_all.10.in_ref, f32[512,1024]{1,0:T(8,128)S(1)} %copy-done, f32[512,1024]{1,0:T(8,128)S(1)} %copy-done.1, f32[8,1024]{1,0:T(8,128)S(1)} %copy-done.4, f32[3,3,1024]{2,1,0:T(4,128)S(1)} %copy-done.3, f32[1,1024]{1,0:T(1,128)S(1)} %bitcast.2), custom_call_target="tpu_custom_call" | custom-call | tf_op jit(solution)/shard_map/join/pallas_call | solution.py:649
  (1 shorter events, 0.0 us)
Async XLA Ops:
  4.3 27.0 %all-to-all-start = ((bf16[32,144,128]{2,1,0:T(8,128)(2,1)}), bf16[32,144,128]{2,1,0:T(8,128)(2,1)S(1)}, u32[]{:S(2)}, u32[]{:S(2)}) async-start(bf16[32,144,128]{2,1,0:T(8,128)(2,1)} %gate.1), calls=%async_computation | async-start | bytes 2359296 | tf_op jit(solution)/shard_map/all_to_all | solution.py:592
  13.7 17.6 %copy-start.2 = (bf16[2048,128]{1,0:T(8,128)(2,1)S(1)}, bf16[2048,128]{1,0:T(8,128)(2,1)}, u32[]{:S(2)}) copy-start(bf16[2048,128]{1,0:T(8,128)(2,1)} %constant.16.clone.table_ref) | copy-start | bytes 1572868
  31.3 31.1 %copy-start.1 = (f32[512,1024]{1,0:T(8,128)S(1)}, f32[512,1024]{1,0:T(8,128)}, u32[]{:S(2)}) copy-start(f32[512,1024]{1,0:T(8,128)} %get-tuple-element.33.s_ref) | copy-start | bytes 6291460
  40.1 22.3 %copy-start = (f32[512,1024]{1,0:T(8,128)S(1)}, f32[512,1024]{1,0:T(8,128)}, u32[]{:S(2)}) copy-start(f32[512,1024]{1,0:T(8,128)} %get-tuple-element.32.q_ref) | copy-start | bytes 6291460
  40.1 22.3 %copy-start.3 = (f32[3,3,1024]{2,1,0:T(4,128)S(1)}, f32[3,3,1024]{2,1,0:T(4,128)}, u32[]{:S(2)}) copy-start(f32[3,3,1024]{2,1,0:T(4,128)} %w_ref.1) | copy-start | bytes 110596
  40.1 22.3 %copy-start.4 = (f32[8,1024]{1,0:T(8,128)S(1)}, f32[8,1024]{1,0:T(8,128)}, u32[]{:S(2)}) copy-start(f32[8,1024]{1,0:T(8,128)} %get-tuple-element.34.ends_ref) | copy-start | bytes 98308
  40.1 22.3 %copy-start.5 = (f32[1024]{0:T(1024)S(1)}, f32[1024]{0:T(1024)}, u32[]{:S(2)}) copy-start(f32[1024]{0:T(1024)} %param.11) | copy-start | bytes 12292

commit v4 on v3

--- a/solution.py
+++ b/solution.py
@@ -200,9 +200,9 @@
     for block in range(blocks):
         tile(block)
         tail(block)
-        if block % 2 == 1:
-            last_copy(block - 1).start()
-            last_copy(block).start()
+        if block % 4 == 3:
+            for at in range(block - 3, block + 1):
+                last_copy(at).start()
     for step in range(steps - 1):
         out_copy(step).wait()
     for block in range(blocks):
@@ -355,18 +355,18 @@
             values.append(jnp.where(is_start, start, value))
         return values
 
-    def first_side(values):
+    def first_side(values, n):
         for pair in range(len(values) // 2):
             high, low = halves(jnp.concatenate(values[2 * pair : 2 * pair + 2], axis=1))
             both = jnp.concatenate([high, low], axis=0)
-            first_raw[pair] = dot(first[: 2 * SIDE], both) + dot(first[2 * SIDE :, :SIDE], high)
-
-    def turn(used=WIDE):
+            first_raw[n % 2, pair] = dot(first[: 2 * SIDE], both) + dot(first[2 * SIDE :, :SIDE], high)
+
+    def turn(n, used=WIDE):
         for at in range(used):
             span = slice(at % 2 * SIDE, (at % 2 + 1) * SIDE)
-            re, im = first_raw[at // 2, :SIDE, span], first_raw[at // 2, SIDE:, span]
+            re, im = first_raw[n % 2, at // 2, :SIDE, span], first_raw[n % 2, at // 2, SIDE:, span]
             store_halves(
-                turned, at, jnp.concatenate([re * cos + im * sin, im * cos - re * sin], axis=1)
+                turned.at[n % 2], at, jnp.concatenate([re * cos + im * sin, im * cos - re * sin], axis=1)
             )
 
     def filter_spectrum(n, spectrum):
@@ -376,30 +376,30 @@
             s_re = spectrum[at * SIDE : (at + 1) * SIDE, :SIDE]
             s_im = spectrum[at * SIDE : (at + 1) * SIDE, SIDE:]
             store_halves(
-                filtered,
+                filtered.at[n % 2],
                 at,
                 jnp.concatenate([s_re * f_re - s_im * f_im, s_re * f_im + s_im * f_re], axis=1),
             )
 
-    def turn_back():
+    def turn_back(n):
         for at in range(WIDE):
-            re = third_raw[at * SIDE : (at + 1) * SIDE, :SIDE]
-            im = third_raw[at * SIDE : (at + 1) * SIDE, SIDE:]
+            re = third_raw[n % 2, at * SIDE : (at + 1) * SIDE, :SIDE]
+            im = third_raw[n % 2, at * SIDE : (at + 1) * SIDE, SIDE:]
             high, low = halves(jnp.concatenate([re * cos - im * sin, im * cos + re * sin], axis=0))
-            unturned[: 2 * SIDE, at * SIDE : (at + 1) * SIDE] = high
-            unturned[2 * SIDE :, at * SIDE : (at + 1) * SIDE] = low
-
-    def first_side_back():
+            unturned[n % 2, : 2 * SIDE, at * SIDE : (at + 1) * SIDE] = high
+            unturned[n % 2, 2 * SIDE :, at * SIDE : (at + 1) * SIDE] = low
+
+    def first_side_back(n):
         for pair in range(WIDE // 2):
             span = slice(2 * pair * SIDE, (2 * pair + 2) * SIDE)
-            done = dot(fourth[...], unturned[: 2 * SIDE, span])
-            fourth_raw[pair] = (
-                done[:SIDE] + done[SIDE:] + dot(fourth[:SIDE], unturned[2 * SIDE :, span])
+            done = dot(fourth[...], unturned[n % 2, : 2 * SIDE, span])
+            fourth_raw[n % 2, pair] = (
+                done[:SIDE] + done[SIDE:] + dot(fourth[:SIDE], unturned[n % 2, 2 * SIDE :, span])
             )
 
     def finish(n, group):
         for i in range(WIDE):
-            value = fourth_raw[i // 2, :, i % 2 * SIDE : (i % 2 + 1) * SIDE]
+            value = fourth_raw[n % 2, i // 2, :, i % 2 * SIDE : (i % 2 + 1) * SIDE]
             top = jnp.max(jnp.max(jnp.abs(value), axis=0, keepdims=True), axis=1, keepdims=True)
             scale = code_scale(top)
             channel = WIDE * n + i
@@ -412,19 +412,19 @@
         if finishes:
             finish(n - 6, finish_group)
         if sides_back:
-            first_side_back()
+            first_side_back(n - 5)
         if turns_back:
-            turn_back()
+            turn_back(n - 4)
         if filters:
-            spectrum = table_right(turned, second)
+            spectrum = table_right(turned.at[n % 2], second)
         if turns:
-            turn()
+            turn(n - 1)
         if filtered_back:
-            third_raw[...] = table_right(filtered, third)
+            third_raw[(n - 3) % 2] = table_right(filtered.at[(n - 3) % 2], third)
         if filters:
             filter_spectrum(n - 2, spectrum)
         if loads:
-            first_side(load(n, load_group))
+            first_side(load(n, load_group), n)
 
     def pack(slot, half):
         group, above = half // 2, half % 2 * 8
@@ -436,9 +436,9 @@
                 code = results[group][place : place + 8, :]
                 out_ref[j, at : at + 8, :] = code.astype(bf16)
 
-    first_side([taps[pl.ds(g, SIDE, stride=groups), :] for g in range(groups)])
-    turn(groups)
-    spectra[...] = table_right(turned, second, groups).reshape(groups, SIDE, 2 * SIDE) * (
+    first_side([taps[pl.ds(g, SIDE, stride=groups), :] for g in range(groups)], -1)
+    turn(-1, groups)
+    spectra[...] = table_right(turned.at[1], second, groups).reshape(groups, SIDE, 2 * SIDE) * (
         1.0 / (SIDE * SIDE)
     )
     for n in range(LAGS - 1):
@@ -628,12 +628,12 @@
             pltpu.VMEM((seq * 8, LANES), f32),
             pltpu.VMEM((SIDE, LANES), f32),
             pltpu.VMEM((SIDE, LANES), f32),
-            pltpu.VMEM((WIDE * SIDE, 4 * SIDE), bf16),
-            pltpu.VMEM((WIDE * SIDE, 4 * SIDE), bf16),
-            pltpu.VMEM((4 * SIDE, WIDE * SIDE), bf16),
-            pltpu.VMEM((WIDE // 2, 2 * SIDE, 2 * SIDE), f32),
-            pltpu.VMEM((WIDE * SIDE, 2 * SIDE), f32),
-            pltpu.VMEM((WIDE // 2, SIDE, 2 * SIDE), f32),
+            pltpu.VMEM((2, WIDE * SIDE, 4 * SIDE), bf16),
+            pltpu.VMEM((2, WIDE * SIDE, 4 * SIDE), bf16),
+            pltpu.VMEM((2, 4 * SIDE, WIDE * SIDE), bf16),
+            pltpu.VMEM((2, WIDE // 2, 2 * SIDE, 2 * SIDE), f32),
+            pltpu.VMEM((2, WIDE * SIDE, 2 * SIDE), f32),
+            pltpu.VMEM((2, WIDE // 2, SIDE, 2 * SIDE), f32),
             pltpu.VMEM((4 * SIDE, 2 * SIDE), bf16),
             pltpu.VMEM((6 * SIDE, 2 * SIDE), bf16),
             pltpu.VMEM((6 * SIDE, 2 * SIDE), bf16),

time: 64.5 us -> 64.5 us (level)
  no operation moved by 1% of the time
where the time goes in v4:
time: 64.5 us; the launch traced here: 64.2 us
  blocking collectives  22.3 us (35%)
  Pallas kernels  21.1 us (33%)
  waiting for transfers between devices  11.4 us (18%)
  starting transfers between devices  8.6 us (13%)
  local copies, waits for them, and re-layouts  0.81 us (1%)
    all_to_all x1, blocking collectives, shards(): message = lax.all_to_all(message, 'seq', 0, 0)  22.3 us
    all_to_all x1, waiting for transfers between devices, shards(): message = lax.all_to_all(message, 'seq', 0, 0)  11.4 us
    pallas_call x1, Pallas kernels, shards(): pl.pallas_call(mix_kernel, in_specs=[whole] * 3, out_specs=hbm, out_shape...  8.75 us
    all_to_all x1, starting transfers between devices, shards(): message = lax.all_to_all(message, 'seq', 0, 0)  8.6 us
    pallas_call x1, Pallas kernels, shards(): pl.pallas_call(local_kernel, in_specs=[whole] * 5, out_specs=[whole] * 3,...  6.17 us
    pallas_call x1, Pallas kernels, shards(): pl.pallas_call(gate_kernel, in_specs=[hbm] * 5, out_specs=hbm, out_shape=...  4.37 us
    pallas_call x1, Pallas kernels, shards(): pl.pallas_call(join_kernel, in_specs=[whole] * 6, out_specs=hbm, out_shap...  1.79 us
  transfers between devices with their start and end apart: 1, of which 1 were waited for; matrix products, arithmetic and copies ran while one was open for 1% of the time, Pallas kernels for 10%

profile of v4, /device:TPU:1, one launch (start us, length us, event | category | flops | bytes accessed | tf_op | source)
XLA Modules:
  0.0 64.2 jit_solution(4957400267631045400)
XLA Ops:
  0.0 4.4 %gate.1 = bf16[32,144,128]{2,1,0:T(8,128)(2,1)} custom-call(bf16[512,1024]{1,0:T(8,128)(2,1)} %q_ref, bf16[512,1024]{1,0:T(8,128)(2,1)} %k_ref, bf16[512,1024]{1,0:T(8,128)(2,1)} %v_ref, f32[3,3,1024]{2,1,0:T(4,128)} %w_ref.1, f32[64,512]{1,0:T(8,128)} %taps_hbm.1), custom_call_target="tpu_custom_call" | custom-call | tf_op jit(solution)/shard_map/gate/pallas_call | solution.py:566
  4.4 8.6 %all-to-all-start = ((bf16[32,144,128]{2,1,0:T(8,128)(2,1)}), bf16[32,144,128]{2,1,0:T(8,128)(2,1)S(1)}, u32[]{:S(2)}, u32[]{:S(2)}) async-start(bf16[32,144,128]{2,1,0:T(8,128)(2,1)} %gate.1), calls=%async_computation | async-start | bytes 2359296 | tf_op jit(solution)/shard_map/all_to_all | solution.py:592
  13.0 0.8 %constant_dynamic-slice_fusion = f32[3,3,32]{2,1,0:T(4,128)S(1)} fusion(f32[3,3,1024]{2,1,0:T(4,128)} %w_ref.1, s32[]{:T(128)S(6)} %select_n.3), kind=kLoop, calls=%fused_computation | loop fusion | bytes 2308 | tf_op jit(solution)/shard_map/dynamic_slice | solution.py:610
  13.8 0.0 copy-start.2
  13.8 6.2 %local.1 = (f32[512,1024]{1,0:T(8,128)}, f32[512,1024]{1,0:T(8,128)}, f32[8,1024]{1,0:T(8,128)}) custom-call(bf16[512,1024]{1,0:T(8,128)(2,1)} %q_ref, bf16[512,1024]{1,0:T(8,128)(2,1)} %k_ref, bf16[512,1024]{1,0:T(8,128)(2,1)} %v_ref, f32[3,3,1024]{2,1,0:T(4,128)} %w_ref.1, f32[1,1024]{1,0:T(1,128)} %bitcast.1), custom_call_target="tpu_custom_call" | custom-call | flops 10485760 | bytes 7340032 | tf_op jit(solution)/shard_map/local/pallas_call | solution.py:594
  19.9 11.4 %all-to-all-done.in_ref = bf16[32,144,128]{2,1,0:T(8,128)(2,1)S(1)} async-done(((bf16[32,144,128]{2,1,0:T(8,128)(2,1)}), bf16[32,144,128]{2,1,0:T(8,128)(2,1)S(1)}, u32[]{:S(2)}, u32[]{:S(2)}) %all-to-all-start) | async-done | bytes 1179680 | tf_op jit(solution)/shard_map/all_to_all | solution.py:592
  31.3 0.0 copy-done.2
  31.3 0.0 copy-start.1
  31.3 8.8 %mix.1 = bf16[32,136,128]{2,1,0:T(8,128)(2,1)S(1)} custom-call(bf16[32,144,128]{2,1,0:T(8,128)(2,1)S(1)} %all-to-all-done.in_ref, f32[3,3,128]{2,1,0:T(4,128)S(1)} %pad.4.w_ref, bf16[2048,128]{1,0:T(8,128)(2,1)S(1)} %copy-done.2), custom_call_target="tpu_custom_call" | custom-call | tf_op jit(solution)/shard_map/mix/pallas_call | solution.py:616
  40.1 0.0 copy-start
  40.1 0.0 copy-start.3
  40.1 0.0 copy-start.4
  40.1 0.0 copy-start.5
  40.2 22.3 %all_to_all.10.in_ref = bf16[32,136,128]{2,1,0:T(8,128)(2,1)S(1)} all-to-all(bf16[32,136,128]{2,1,0:T(8,128)(2,1)S(1)} %mix.1), channel_id=1, replica_groups=mesh['seq'=32,'ch'=8] {'seq'}, dimensions={0} | all-to-all | bytes 2228224 | tf_op jit(solution)/shard_map/all_to_all | solution.py:647
  62.4 0.0 copy-done.1
  62.4 0.0 copy-done
  62.4 0.0 copy-done.3
  62.4 0.0 copy-done.4
  62.4 0.0 copy-done.5
  62.4 1.8 %join.1 = bf16[512,1024]{1,0:T(8,128)(2,1)} custom-call(bf16[32,136,128]{2,1,0:T(8,128)(2,1)S(1)} %all_to_all.10.in_ref, f32[512,1024]{1,0:T(8,128)S(1)} %copy-done, f32[512,1024]{1,0:T(8,128)S(1)} %copy-done.1, f32[8,1024]{1,0:T(8,128)S(1)} %copy-done.4, f32[3,3,1024]{2,1,0:T(4,128)S(1)} %copy-done.3, f32[1,1024]{1,0:T(1,128)S(1)} %bitcast.2), custom_call_target="tpu_custom_call" | custom-call | tf_op jit(solution)/shard_map/join/pallas_call | solution.py:649
  (1 shorter events, 0.0 us)
Async XLA Ops:
  4.4 27.0 %all-to-all-start = ((bf16[32,144,128]{2,1,0:T(8,128)(2,1)}), bf16[32,144,128]{2,1,0:T(8,128)(2,1)S(1)}, u32[]{:S(2)}, u32[]{:S(2)}) async-start(bf16[32,144,128]{2,1,0:T(8,128)(2,1)} %gate.1), calls=%async_computation | async-start | bytes 2359296 | tf_op jit(solution)/shard_map/all_to_all | solution.py:592
  13.8 17.6 %copy-start.2 = (bf16[2048,128]{1,0:T(8,128)(2,1)S(1)}, bf16[2048,128]{1,0:T(8,128)(2,1)}, u32[]{:S(2)}) copy-start(bf16[2048,128]{1,0:T(8,128)(2,1)} %constant.16.clone.table_ref) | copy-start | bytes 1572868
  31.3 31.1 %copy-start.1 = (f32[512,1024]{1,0:T(8,128)S(1)}, f32[512,1024]{1,0:T(8,128)}, u32[]{:S(2)}) copy-start(f32[512,1024]{1,0:T(8,128)} %get-tuple-element.33.s_ref) | copy-start | bytes 6291460
  40.1 22.3 %copy-start = (f32[512,1024]{1,0:T(8,128)S(1)}, f32[512,1024]{1,0:T(8,128)}, u32[]{:S(2)}) copy-start(f32[512,1024]{1,0:T(8,128)} %get-tuple-element.32.q_ref) | copy-start | bytes 6291460
  40.1 22.3 %copy-start.3 = (f32[3,3,1024]{2,1,0:T(4,128)S(1)}, f32[3,3,1024]{2,1,0:T(4,128)}, u32[]{:S(2)}) copy-start(f32[3,3,1024]{2,1,0:T(4,128)} %w_ref.1) | copy-start | bytes 110596
  40.1 22.3 %copy-start.4 = (f32[8,1024]{1,0:T(8,128)S(1)}, f32[8,1024]{1,0:T(8,128)}, u32[]{:S(2)}) copy-start(f32[8,1024]{1,0:T(8,128)} %get-tuple-element.34.ends_ref) | copy-start | bytes 98308
  40.1 22.3 %copy-start.5 = (f32[1024]{0:T(1024)S(1)}, f32[1024]{0:T(1024)}, u32[]{:S(2)}) copy-start(f32[1024]{0:T(1024)} %param.11) | copy-start | bytes 12292
